TPU v7x, 256 devices: a whole 4x4x8 slice. The times are simulated.
256 devices in a mesh: row: 8 (over x, y_hi), col: 4 (over y_lo, core), dp: 8 (over z).
Axes of the slice: x: 4, y: 4 (y_hi: 2, y_lo: 2; y = y_hi * 2 + y_lo), z: 8, core: 2. Of those that a mesh axis runs over, the one named last changes fastest.
Arguments:
- qkv: bfloat16 [8, 192, 96, 3072], P('dp', 'row', 'col'), may hold values from -64 to 64, as said below
- grad_out: bfloat16 [8, 192, 96, 1024], P('dp', 'row', 'col'), may hold values from -6 to 6
- w_qkv: bfloat16 [1024, 3072], P('dp'), may hold values from -0.1875 to 0.1875
- w_proj: bfloat16 [1024, 1024], replicated, may hold values from -0.1875 to 0.1875
- norm_gain: float32 [1024], replicated, may hold values from 0.5 to 1.5
- region: int32 [192, 96], P('row', 'col'), may hold values from 0 to 3
Outputs:
- grad_in: bfloat16 [8, 192, 96, 1024], P('dp', 'row', 'col')
- grad_proj: float32 [1024, 1024], P(('row', 'col', 'dp'))
- grad_gain: float32 [1024], replicated
Inputs may be any that keep to these rules, and one draw needn't show every extreme that they name: `qkv`: entries of the saved projections are finite reals.
All inputs are finite; a program needn't handle non-finite values.
Results may differ from a plain program's by a relative error of at most 0.013.
Values may be sent and summed in bfloat16 or wider, within the bound.
No kernel may reach another device: no remote copies, remote signals or barrier semaphores. Data moves between devices by JAX's collectives and lax.ppermute only.
A program may use at most 128 MiB of HBM per device.

v0:
```python
import math

import jax
import jax.numpy as jnp
from jax import lax
from jax.experimental import pallas as pl
from jax.experimental.pallas import tpu as pltpu
from jax.sharding import PartitionSpec as P

HEADS = 32
GROUP = 4
BF = jnp.bfloat16
F32 = jnp.float32
NT = (((1,), (1,)), ((), ()))
TN = (((0,), (0,)), ((), ()))
LIMIT = 56 * 2**20
GAIN_ROWS = 8
RADIX = 4
REGIONS = 4


def params():
    return pltpu.CompilerParams(vmem_limit_bytes=LIMIT)


def shape(*dims):
    return lambda kind: jax.ShapeDtypeStruct(dims, kind)


def split3(value):
    high = value.astype(BF)
    rest = value - high.astype(F32)
    mid = rest.astype(BF)
    return high, mid, (rest - mid.astype(F32)).astype(BF)


def forward_kernel(q_ref, k_ref, v_ref, hot_ref, p_ref, o_ref, inv_ref):
    tokens, lanes = q_ref.shape
    size = lanes // GROUP
    factor = size ** (-0.5) * math.log2(math.e)
    queries, keys, values, hot = q_ref[...], k_ref[...], v_ref[...], hot_ref[...]
    lane = lax.broadcasted_iota(jnp.int32, (tokens, lanes), 1)
    head = lane // size
    mask = jnp.where(lane % size < REGIONS, (hot.astype(F32) - 1.0) * 1e30, 0.0).astype(BF)

    def scores_of(h):
        left, right = jnp.where(head == h, queries, hot), jnp.where(head == h, keys, mask)
        return lax.dot_general(left, right, NT, preferred_element_type=F32)

    def attend(h, expo):
        summed = jnp.where(head == h, values, jnp.ones_like(values))
        both = jnp.dot(expo, summed, preferred_element_type=F32)
        inv = 1.0 / pltpu.roll(both, size, axis=1)
        return both * inv, inv

    scores = scores_of(0)
    last, out, inverse = None, None, None
    for h in range(GROUP + 1):
        ahead = scores_of(h + 1) if h + 1 < GROUP else None
        if last is not None:
            attn, inv = attend(h - 1, last)
            out = attn if out is None else jnp.where(head == h - 1, attn, out)
            inverse = inv if inverse is None else jnp.where(head == h - 1, inv, inverse)
        if h < GROUP:
            top = jnp.max(scores, axis=1, keepdims=True)
            last = jnp.exp2((scores - top) * factor).astype(BF)
            p_ref[h] = last
        scores = ahead
    o_ref[...] = out
    inv_ref[...] = inverse


def backward_kernel(p_ref, q_ref, k_ref, v_ref, do_ref, o_ref, inv_ref, dq_ref, dk_ref, dv_ref):
    tokens, lanes = q_ref.shape
    size = lanes // GROUP
    scale = size ** (-0.5)
    keys, values, dout, inv = k_ref[...], v_ref[...], do_ref[...], inv_ref[...]
    lane = lax.broadcasted_iota(jnp.int32, (tokens, lanes), 1)
    head = lane // size
    dout_f = dout.astype(F32)
    row_i = lax.broadcasted_iota(jnp.int32, (lanes, lanes), 0) // size
    col_i = lax.broadcasted_iota(jnp.int32, (lanes, lanes), 1)
    pick = jnp.where((col_i // size == (row_i + 1) % GROUP) & (col_i % size < 3), 1.0, 0.0).astype(BF)
    parts = jnp.concatenate(split3(dout_f * o_ref[...]), axis=1)
    delta = jnp.dot(parts, jnp.concatenate([pick] * 3, axis=0), preferred_element_type=F32)
    d_high = delta.astype(BF).astype(F32)
    d_rest = delta - d_high
    d_mid = d_rest.astype(BF).astype(F32)
    which = lane % size
    columns = jnp.where(
        which == 0, d_high, jnp.where(which == 1, d_mid, jnp.where(which == 2, d_rest - d_mid, 0.0))
    ).astype(BF)
    dout_t = (dout_f * inv).T.astype(BF)
    query_t = (q_ref[...].astype(F32) * (inv * scale)).T.astype(BF)

    def dprobs_of(h):
        minus = jnp.where((head == (h + 1) % GROUP) & (which < 3), -1.0, 0.0).astype(BF)
        left, right = jnp.where(head == h, dout, columns), jnp.where(head == h, values, minus)
        return lax.dot_general(left, right, NT, preferred_element_type=F32)

    dprobs = dprobs_of(0)
    dq, dks, dvs = None, [], []
    for h in range(GROUP):
        ahead = dprobs_of(h + 1) if h + 1 < GROUP else None
        probs = p_ref[h]
        dscores = (probs.astype(F32) * dprobs).astype(BF)
        part = jnp.dot(dscores, keys, preferred_element_type=F32)
        dq = part if dq is None else jnp.where(head == h, part, dq)
        rows = slice(size * h, size * (h + 1))
        dks.append(jnp.dot(query_t[rows], dscores, preferred_element_type=F32))
        dvs.append(jnp.dot(dout_t[rows], probs, preferred_element_type=F32))
        dprobs = ahead
    dq_ref[...] = (dq * (inv * scale)).astype(BF)
    dk_ref[...] = jnp.concatenate(dks, axis=0).T.astype(BF)
    dv_ref[...] = jnp.concatenate(dvs, axis=0).T.astype(BF)


def column_block(tokens, offset):
    return pl.BlockSpec((tokens, 128), lambda g: (0, g + offset))


def forward(qkv, hot, first, count):
    tokens = qkv.shape[0]
    per = qkv.shape[1] // 3 // 128
    whole = pl.BlockSpec((tokens, 128), lambda g: (0, 0))
    out = shape(tokens, count * 128)(F32)
    return pl.pallas_call(
        forward_kernel,
        grid=(count,),
        in_specs=[column_block(tokens, first + per * i) for i in range(3)] + [whole],
        out_specs=[pl.BlockSpec((GROUP, tokens, tokens), lambda g: (g, 0, 0))]
        + [column_block(tokens, 0)] * 2,
        out_shape=[shape(count * GROUP, tokens, tokens)(BF), out, out],
        compiler_params=params(),
        cost_estimate=pl.CostEstimate(
            flops=count * 3_200_000_000, bytes_accessed=count * 4_000_000, transcendentals=0
        ),
        name="attn_forward",
    )(qkv, qkv, qkv, hot)


def backward(probs, qkv, dattn, out, inverse, first, count):
    tokens = qkv.shape[0]
    per = qkv.shape[1] // 3 // 128
    return pl.pallas_call(
        backward_kernel,
        grid=(count,),
        in_specs=[pl.BlockSpec((GROUP, tokens, tokens), lambda g: (g + first, 0, 0))]
        + [column_block(tokens, first + per * i) for i in range(3)]
        + [column_block(tokens, first)] * 3,
        out_specs=[column_block(tokens, 0)] * 3,
        out_shape=[shape(tokens, count * 128)(BF)] * 3,
        compiler_params=params(),
        cost_estimate=pl.CostEstimate(
            flops=count * 3_600_000_000, bytes_accessed=count * 4_000_000, transcendentals=0
        ),
        name="attn_backward",
    )(probs, qkv, qkv, qkv, dattn, out, inverse)


def pack_gain(high, low):
    rows = lax.broadcasted_iota(jnp.int32, (GAIN_ROWS, high.shape[1]), 0)
    return jnp.where(rows == 0, high, jnp.where(rows == 1, low, 0.0)).astype(BF)


def middle_kernel(order, bit_ref, *refs):
    outs, (w_ref, dz_ref, gain_ref, do_ref, send_ref, keep_ref, term_ref, sums) = refs[:-8], refs[-8:]
    attn = jnp.concatenate([ref[...].astype(BF) for ref in outs], axis=1)
    weights = w_ref[...]
    proj = jnp.dot(attn, weights, preferred_element_type=F32)
    centred = proj - jnp.mean(proj, axis=1, keepdims=True)
    rstd = lax.rsqrt(jnp.mean(centred * centred, axis=1, keepdims=True) + 1e-05)
    normed = centred * rstd
    dz = dz_ref[...].astype(F32)
    term = jnp.sum(dz * normed, axis=0, keepdims=True)
    scaled = dz * gain_ref[...]
    mean = jnp.mean(scaled, axis=1, keepdims=True)
    dot = jnp.mean(scaled * normed, axis=1, keepdims=True)
    dproj = (rstd * (scaled - mean - normed * dot)).astype(BF)
    do_ref[...] = lax.dot_general(dproj, weights, NT, preferred_element_type=F32).astype(BF)
    sums[...] = lax.dot_general(attn, dproj, TN, preferred_element_type=F32)
    half = len(order) // 2
    size = sums.shape[0] // len(order)
    low, high = (
        jnp.concatenate([sums[size * b : size * (b + 1)] for b in part], axis=0)
        for part in (order[:half], order[half:])
    )
    second = bit_ref[0] == 1
    term_high = term.astype(BF).astype(F32)
    term_low = (term - term_high).astype(BF).astype(F32)
    send_ref[0:GAIN_ROWS] = pack_gain(term_high, term_low)
    send_ref[GAIN_ROWS:] = jnp.where(second, low, high).astype(BF)
    keep_ref[...] = jnp.where(second, high, low)
    term_ref[...] = term_high + term_low


def middle(outs, w_proj, dz, gain, bit, order):
    tokens, width = dz.shape
    vmem = pl.BlockSpec(memory_space=pltpu.VMEM)
    half = width // 2
    return pl.pallas_call(
        lambda *refs: middle_kernel(order, *refs),
        in_specs=[pl.BlockSpec(memory_space=pltpu.SMEM)] + [vmem] * (len(outs) + 3),
        out_specs=[vmem] * 4,
        out_shape=[
            shape(tokens, width)(BF),
            shape(GAIN_ROWS + half, width)(BF),
            shape(half, width)(F32),
            shape(1, width)(F32),
        ],
        scratch_shapes=[pltpu.VMEM((width, width), F32)],
        compiler_params=params(),
        cost_estimate=pl.CostEstimate(
            flops=8_000_000_000, bytes_accessed=16_000_000, transcendentals=0
        ),
        name="middle",
    )(bit, *outs, w_proj, dz, gain[None])


def back_kernel(core_ref, *refs):
    parts, (mine_ref, other_ref), outs = refs[:6], refs[6:8], refs[8:]
    first = core_ref[0] == 0
    left = jnp.concatenate([ref[...] for ref in parts], axis=1)
    rows = 64
    blocks = []
    for z in range(mine_ref.shape[0] // rows):
        mine, other = mine_ref[rows * z : rows * (z + 1)], other_ref[rows * z : rows * (z + 1)]
        blocks += [jnp.where(first, mine, other), jnp.where(first, other, mine)]
    total = lax.dot_general(left, jnp.concatenate(blocks, axis=0), NT, preferred_element_type=F32)
    side = math.isqrt(total.shape[0])
    half = side // 2
    for n, ref in enumerate(outs):
        start = side * half * (n // 2) + half * (n % 2)
        ref[...] = jnp.concatenate(
            [total[start + side * i : start + side * i + half] for i in range(half)], axis=0
        ).astype(BF)


def back_product(parts, mine, other, core, which):
    tokens = parts[0].shape[0]
    rows, inner = mine.shape
    steps = 2
    wide = 2 * rows // (2 * steps)
    side = pl.BlockSpec((rows // (2 * steps), inner), lambda g: (g + which * steps, 0))
    out = pl.BlockSpec((tokens // 4, wide), lambda g: (0, g))
    return pl.pallas_call(
        back_kernel,
        grid=(steps,),
        in_specs=[pl.BlockSpec(memory_space=pltpu.SMEM)]
        + [pl.BlockSpec(part.shape, lambda g: (0, 0)) for part in parts]
        + [side] * 2,
        out_specs=[out] * 4,
        out_shape=[shape(tokens // 4, wide * steps)(BF)] * 4,
        compiler_params=params(),
        cost_estimate=pl.CostEstimate(
            flops=2_500_000_000, bytes_accessed=8_000_000, transcendentals=0
        ),
        name="back_product",
    )(core, *parts, mine, other)


def position(row, col):
    return row // 2, row % 2 * 2 + col // 2, col % 2


def place(x, y, core):
    return x * 2 + y // 2, y % 2 * 2 + core


def block_order(row_count, col_count):
    order = []
    for core in range(2):
        for first in range(RADIX):
            for second in range(RADIX):
                x, y = (first, second) if core == 0 else (second, first)
                row, col = place(x, y, core)
                order.append(row * col_count + col)
    return order


def plane_pairs(rows, cols, turn, step):
    pairs = []
    for r in range(rows):
        for c in range(cols):
            x, y, core = position(r, c)
            if core == turn:
                x = (x + step) % RADIX
            else:
                y = (y + step) % RADIX
            to_r, to_c = place(x, y, core)
            pairs.append((r * cols + c, to_r * cols + to_c))
    return pairs


def round_pieces(total, gain, index, count):
    rows = total.shape[0] // count
    high = lax.reduce_precision(gain, 8, 7)
    low = lax.reduce_precision(gain - high, 8, 7)
    packed = pack_gain(high, low)
    pieces = [
        jnp.concatenate(
            [
                packed,
                lax.dynamic_slice_in_dim(total, (index + n) % count * rows, rows, 0).astype(BF),
            ],
            axis=0,
        )
        for n in range(1, count)
    ]
    return pieces, lax.dynamic_slice_in_dim(total, index * rows, rows, 0), high + low


def round_sums(got, own, gain, index):
    count = len(got) + 1
    gains = [gain]
    for value in got:
        own = own + value[GAIN_ROWS:].astype(F32)
        gains.append(value[0:1].astype(F32) + value[1:2].astype(F32))
    turned = jnp.concatenate(gains[::-1] * 2, axis=0)
    ordered = lax.dynamic_slice_in_dim(turned, count - 1 - index, count, 0)
    gain = ordered[0:1]
    for n in range(1, count):
        gain = gain + ordered[n : n + 1]
    return own, gain


def shift(value, rows, cols, step):
    r, c = lax.axis_size("row"), lax.axis_size("col")
    if rows and cols:
        pairs = [
            (i * c + j, (i + step) % r * c + (j + step) % c) for i in range(r) for j in range(c)
        ]
        return lax.ppermute(value, ("row", "col"), pairs)
    name, count = ("row", r) if rows else ("col", c)
    return lax.ppermute(value, name, [(i, (i + step) % count) for i in range(count)])


def quadrant(values, low_row, low_col):
    half = values.shape[0] // 2
    rows = slice(0, half) if low_row else slice(half, None)
    cols = slice(0, half) if low_col else slice(half, None)
    return values[rows, cols]


def per_device(qkv, grad_out, w_qkv, w_proj, norm_gain, region):
    side, width = grad_out.shape[1], grad_out.shape[3]
    half = side // 2
    tokens = side * side
    grad = grad_out[0]
    flat = (half * half, width)
    square = (half, half, width)

    def send(value, rows, cols, step):
        return shift(value.reshape(flat), rows, cols, step).reshape(square)

    core = lax.axis_index("col") % 2
    rows = w_qkv.shape[0] // 2
    mine_w = lax.dynamic_slice_in_dim(w_qkv, core * rows, rows, 0)
    mine = lax.all_gather(mine_w, "dp", axis=0, tiled=True)
    from_row = send(quadrant(grad, True, False), True, False, -1)
    from_col = send(quadrant(grad, False, True), False, True, -1)
    from_both = send(quadrant(grad, True, True), True, True, -1)

    ids = region.reshape(tokens, 1)
    lane = lax.broadcasted_iota(jnp.int32, (tokens, 128), 1)
    hot = (ids == lane % (width // HEADS)).astype(BF)
    qkv_t = qkv.reshape(tokens, 3 * width)
    groups = width // 128
    qkv_t, mine_w = lax.optimization_barrier((qkv_t, mine_w))
    probs, out, inverse = forward(qkv_t, hot, 0, groups)

    dz = jnp.concatenate(
        [
            jnp.concatenate([quadrant(grad, False, False), from_col], axis=1),
            jnp.concatenate([from_row, from_both], axis=1),
        ],
        axis=0,
    ).reshape(tokens, width)

    r, c, d = lax.axis_size("row"), lax.axis_size("col"), lax.axis_size("dp")
    row, col, dp = lax.axis_index("row"), lax.axis_index("col"), lax.axis_index("dp")
    bit = core.astype(jnp.int32).reshape(1)
    dattn, wire, keep, gain = middle([out], w_proj, dz, norm_gain, bit, block_order(r, c))
    other = lax.ppermute(mine, "col", [(i, i ^ 1) for i in range(c)])
    norm = (tokens * r * c * d) ** (-0.5)
    got = lax.ppermute(wire, "col", [(i, i ^ 1) for i in range(c)])
    x, y, _ = position(row, col)

    def plane_round(pieces, turn):
        return [
            lax.ppermute(piece, ("row", "col"), plane_pairs(r, c, turn, n + 1))
            for n, piece in enumerate(pieces)
        ]

    half_groups = groups // 2
    early = backward(probs, qkv_t, dattn, out, inverse, 0, half_groups)
    early, got = lax.optimization_barrier((early, got))
    sums = keep + got[GAIN_ROWS:].astype(F32)
    gain = gain + (got[0:1].astype(F32) + got[1:2].astype(F32))
    index = jnp.where(core == 0, x, y)
    pieces, own, gain = round_pieces(sums, gain, index, RADIX)
    dattn, pieces = lax.optimization_barrier((dattn, pieces))
    got = plane_round(pieces, 0)

    late = backward(probs, qkv_t, dattn, out, inverse, half_groups, half_groups)
    late, got = lax.optimization_barrier((late, got))
    sums, gain = round_sums(got, own, gain, index)
    index = jnp.where(core == 0, y, x)
    pieces, own, gain = round_pieces(sums, gain, index, RADIX)
    late, pieces = lax.optimization_barrier((late, pieces))
    got = plane_round(pieces, 1)

    parts = [part for pair in zip(early, late) for part in pair]
    moved = []
    for n in range(2):
        quarters = back_product(parts, mine, other, bit, n)
        if n == 1:
            quarters, got = lax.optimization_barrier((quarters, got))
        moved.append(
            [quarters[0]] + [shift(quarters[i], i // 2 == 1, i % 2 == 1, 1) for i in (1, 2, 3)]
        )

    sums, gain = round_sums(got, own, gain, index)
    pieces, own, gain = round_pieces(sums, gain, dp, d)
    got = [
        lax.ppermute(piece, "dp", [(i, (i + n + 1) % d) for i in range(d)])
        for n, piece in enumerate(pieces)
    ]
    sums, gain = round_sums(got, own, gain, dp)
    grad_proj, grad_gain = sums * norm, gain * norm

    local, to_col, to_row, to_both = (
        jnp.concatenate(pair, axis=1).reshape(square) for pair in zip(*moved)
    )
    moved = jnp.concatenate(
        [
            jnp.concatenate([to_both, to_row], axis=1),
            jnp.concatenate([to_col, local], axis=1),
        ],
        axis=0,
    )
    grad_in = (grad.astype(F32) + moved.astype(F32)).astype(BF)[None]
    return (grad_in, grad_proj, grad_gain[0])


def solution(mesh):
    return jax.shard_map(
        per_device,
        mesh=mesh,
        in_specs=(
            P("dp", "row", "col", None),
            P("dp", "row", "col", None),
            P("dp", None),
            P(),
            P(),
            P("row", "col"),
        ),
        out_specs=(P("dp", "row", "col", None), P(("row", "col", "dp"), None), P()),
        check_vma=False,
    )
```

profile of v0, /device:TPU:1, one launch (start us, length us, event | category | flops | bytes accessed | tf_op | source)
XLA Modules:
  0.0 150.4 jit_solution(11582430456111448076)
XLA Ops:
  7.2 1.7 %fusion.24 = (bf16[12,12,1024]{2,1,0:T(8,128)(2,1)S(1)}, bf16[12,12,1024]{2,1,0:T(8,128)(2,1)S(1)}, bf16[12,12,1024]{2,1,0:T(8,128)(2,1)S(1)}, bf16[12,12,1024]{2,1,0:T(8,128)(2,1)S(1)}) fusion(bf16[24,24,1024]{2,1,0:T(8,128)(2,1)} %bitcast.16), kind=kLoop, calls=%fused_computation.113 | loop fusion | bytes 2359296 | tf_op jit(solution)/shard_map/slice | solution.py:342
  9.0 3.3 %collective-permute-start = (bf16[144,1024]{1,0:T(8,128)(2,1)S(1)}, bf16[144,1024]{1,0:T(8,128)(2,1)S(1)}, u32[]{:S(2)}, u32[]{:S(2)}) collective-permute-start(bf16[144,1024]{1,0:T(8,128)(2,1)S(1)} %reshape.78), channel_id=1, source_target_pairs={{0,24},{8,0},{16,8},{24,16},{1,25},{9,1},{17,9},{25,17},{2,26},{10... | collective-permute-start | bytes 884744 | tf_op jit(solution)/shard_map/ppermute | solution.py:335
  12.4 3.5 %collective-permute-start.1 = (bf16[144,1024]{1,0:T(8,128)(2,1)S(1)}, bf16[144,1024]{1,0:T(8,128)(2,1)S(1)}, u32[]{:S(2)}, u32[]{:S(2)}) collective-permute-start(bf16[144,1024]{1,0:T(8,128)(2,1)S(1)} %reshape.80), channel_id=1, source_target_pairs={{0,224},{32,0},{64,32},{96,64},{128,96},{160,128},{192,160},{224,1... | collective-permute-start | bytes 884744 | tf_op jit(solution)/shard_map/ppermute | solution.py:335
  15.9 1.3 collective-permute-start.2
  19.0 22.4 %attn_forward.1 = (bf16[32,576,576]{2,1,0:T(8,128)(2,1)}, f32[576,1024]{1,0:T(8,128)}, f32[576,1024]{1,0:T(8,128)}) custom-call(bf16[576,3072]{1,0:T(8,128)(2,1)} %bitcast.25, bf16[576,3072]{1,0:T(8,128)(2,1)} %bitcast.26, bf16[576,3072]{1,0:T(8,128)(2,1)} %bitcast.27, bf16[576,128]{1,0:T(8,128)(2,1)} %fusion.hot_ref), custom_call_target="tpu_custom_call" | custom-call | flops 25600000000 | bytes 32000000 | tf_op jit(solution)/shard_map/attn_forward/pallas_call | solution.py:127
  41.7 1.4 maximum_maximum_fusion
  43.0 9.7 %middle.1 = (bf16[576,1024]{1,0:T(8,128)(2,1)}, bf16[520,1024]{1,0:T(8,128)(2,1)}, f32[512,1024]{1,0:T(8,128)}, f32[1,1024]{1,0:T(1,128)}) custom-call(s32[1]{0:T(128)} %bitcast.refs_0_.core_ref, f32[576,1024]{1,0:T(8,128)} %get-tuple-element.54.refs_1_.o_ref, bf16[1024,1024]{1,0:T(8,128)(2,1)} %refs_2_.1, bf16[576,1024]{1,0:T(8,128)(2,1)} %bitcast.17, ...), custom_call_target="tpu_custom_call" | custom-call | flops 8000000000 | bytes 16000000 | tf_op jit(solution)/shard_map/middle/pallas_call | solution.py:201
  52.7 14.6 %attn_backward.2 = (bf16[576,512]{1,0:T(8,128)(2,1)}, bf16[576,512]{1,0:T(8,128)(2,1)}, bf16[576,512]{1,0:T(8,128)(2,1)}) custom-call(bf16[32,576,576]{2,1,0:T(8,128)(2,1)} %get-tuple-element.53.p_ref, bf16[576,3072]{1,0:T(8,128)(2,1)} %bitcast.28, bf16[576,3072]{1,0:T(8,128)(2,1)} %bitcast.29, bf16[576,3072]{1,0:T(8,128)(2,1)} %bitcast.30, ...), custom_call_target="tpu_custom_call" | custom-call | flops 14400000000 | bytes 16000000 | tf_op jit(solution)/shard_map/attn_backward/pallas_call | solution.py:145
  69.5 2.8 %collective-permute-start.5 = (bf16[136,1024]{1,0:T(8,128)(2,1)S(1)}, bf16[136,1024]{1,0:T(8,128)(2,1)S(1)}, u32[]{:S(2)}, u32[]{:S(2)}) collective-permute-start(bf16[136,1024]{1,0:T(8,128)(2,1)S(1)} %get-tuple-element.70), channel_id=1, source_target_pairs={{0,128},{8,40},{16,144},{24,56},{32,160},{40,8},{48,176},{56,24},{... | collective-permute-start | bytes 835592 | tf_op jit(solution)/shard_map/ppermute | solution.py:391
  72.3 1.6 %collective-permute-start.6 = (bf16[136,1024]{1,0:T(8,128)(2,1)S(1)}, bf16[136,1024]{1,0:T(8,128)(2,1)S(1)}, u32[]{:S(2)}, u32[]{:S(2)}) collective-permute-start(bf16[136,1024]{1,0:T(8,128)(2,1)S(1)} %get-tuple-element.71), channel_id=1, source_target_pairs={{0,192},{8,56},{16,208},{24,8},{32,224},{40,24},{48,240},{56,40},{... | collective-permute-start | bytes 835592 | tf_op jit(solution)/shard_map/ppermute | solution.py:391
  73.9 14.5 %attn_backward.3 = (bf16[576,512]{1,0:T(8,128)(2,1)}, bf16[576,512]{1,0:T(8,128)(2,1)}, bf16[576,512]{1,0:T(8,128)(2,1)}) custom-call(bf16[32,576,576]{2,1,0:T(8,128)(2,1)} %get-tuple-element.53.p_ref, bf16[576,3072]{1,0:T(8,128)(2,1)} %bitcast.31, bf16[576,3072]{1,0:T(8,128)(2,1)} %bitcast.32, bf16[576,3072]{1,0:T(8,128)(2,1)} %bitcast.33, ...), custom_call_target="tpu_custom_call" | custom-call | flops 14400000000 | bytes 16000000 | tf_op jit(solution)/shard_map/attn_backward/pallas_call | solution.py:145
  90.9 5.4 %back_product.3 = (bf16[144,512]{1,0:T(8,128)(2,1)}, bf16[144,512]{1,0:T(8,128)(2,1)}, bf16[144,512]{1,0:T(8,128)(2,1)}, bf16[144,512]{1,0:T(8,128)(2,1)}) custom-call(s32[1]{0:T(128)} %bitcast.refs_0_.core_ref, bf16[576,512]{1,0:T(8,128)(2,1)} %get-tuple-element.61.refs_0_, bf16[576,512]{1,0:T(8,128)(2,1)} %get-tuple-element.78.refs_1_, ...), custom_call_target="tpu_custom_call" | custom-call | flops 2500000000 | bytes 8000000 | tf_op jit(solution)/shard_map/back_product/pallas_call | solution.py:246
  96.7 1.9 %collective-permute-start.17 = (bf16[12,1024]{1,0:T(8,128)(2,1)S(1)}, bf16[12,1024]{1,0:T(8,128)(2,1)S(1)}, u32[]{:S(2)}, u32[]{:S(2)}) collective-permute-start(bf16[12,1024]{1,0:T(8,128)(2,1)S(1)} %get-tuple-element.124), channel_id=1, source_target_pairs={{0,1},{1,2},{2,3},{3,4},{4,5},{5,6},{6,7},{7,0},{8,9},{9,10},{10,1... | collective-permute-start | bytes 73736 | tf_op jit(solution)/shard_map/ppermute | solution.py:426
  98.7 3.0 %collective-permute-start.18 = (bf16[12,1024]{1,0:T(8,128)(2,1)S(1)}, bf16[12,1024]{1,0:T(8,128)(2,1)S(1)}, u32[]{:S(2)}, u32[]{:S(2)}) collective-permute-start(bf16[12,1024]{1,0:T(8,128)(2,1)S(1)} %get-tuple-element.125), channel_id=1, source_target_pairs={{0,2},{1,3},{2,4},{3,5},{4,6},{5,7},{6,0},{7,1},{8,10},{9,11},{10,... | collective-permute-start | bytes 73736 | tf_op jit(solution)/shard_map/ppermute | solution.py:426
  101.7 3.8 %collective-permute-start.19 = (bf16[12,1024]{1,0:T(8,128)(2,1)S(1)}, bf16[12,1024]{1,0:T(8,128)(2,1)S(1)}, u32[]{:S(2)}, u32[]{:S(2)}) collective-permute-start(bf16[12,1024]{1,0:T(8,128)(2,1)S(1)} %get-tuple-element.126), channel_id=1, source_target_pairs={{0,3},{1,4},{2,5},{3,6},{4,7},{5,0},{6,1},{7,2},{8,11},{9,12},{10,... | collective-permute-start | bytes 73736 | tf_op jit(solution)/shard_map/ppermute | solution.py:426
  105.9 4.5 %collective-permute-start.21 = (bf16[12,1024]{1,0:T(8,128)(2,1)S(1)}, bf16[12,1024]{1,0:T(8,128)(2,1)S(1)}, u32[]{:S(2)}, u32[]{:S(2)}) collective-permute-start(bf16[12,1024]{1,0:T(8,128)(2,1)S(1)} %get-tuple-element.128), channel_id=1, source_target_pairs={{0,5},{1,6},{2,7},{3,0},{4,1},{5,2},{6,3},{7,4},{8,13},{9,14},{10,... | collective-permute-start | bytes 73736 | tf_op jit(solution)/shard_map/ppermute | solution.py:426
  110.4 5.4 %back_product.2 = (bf16[144,512]{1,0:T(8,128)(2,1)}, bf16[144,512]{1,0:T(8,128)(2,1)}, bf16[144,512]{1,0:T(8,128)(2,1)}, bf16[144,512]{1,0:T(8,128)(2,1)}) custom-call(s32[1]{0:T(128)} %bitcast.refs_0_.core_ref, bf16[576,512]{1,0:T(8,128)(2,1)} %get-tuple-element.61.refs_0_, bf16[576,512]{1,0:T(8,128)(2,1)} %get-tuple-element.78.refs_1_, ...), custom_call_target="tpu_custom_call" | custom-call | flops 2500000000 | bytes 8000000 | tf_op jit(solution)/shard_map/back_product/pallas_call | solution.py:246
  117.0 2.4 %collective-permute-start.22 = (bf16[12,1024]{1,0:T(8,128)(2,1)S(1)}, bf16[12,1024]{1,0:T(8,128)(2,1)S(1)}, u32[]{:S(2)}, u32[]{:S(2)}) collective-permute-start(bf16[12,1024]{1,0:T(8,128)(2,1)S(1)} %get-tuple-element.129), channel_id=1, source_target_pairs={{0,6},{1,7},{2,0},{3,1},{4,2},{5,3},{6,4},{7,5},{8,14},{9,15},{10,... | collective-permute-start | bytes 73736 | tf_op jit(solution)/shard_map/ppermute | solution.py:426
  120.3 4.9 %collective-permute-start.8 = (bf16[144,512]{1,0:T(8,128)(2,1)S(1)}, bf16[144,512]{1,0:T(8,128)(2,1)S(1)}, u32[]{:S(2)}, u32[]{:S(2)}) collective-permute-start(bf16[144,512]{1,0:T(8,128)(2,1)S(1)} %copy-done.12), channel_id=1, source_target_pairs={{0,40},{8,48},{16,56},{24,32},{32,72},{40,80},{48,88},{56,64},{64,... | collective-permute-start | bytes 442376 | tf_op jit(solution)/shard_map/ppermute | solution.py:333
  126.2 2.7 %collective-permute-start.14 = (bf16[144,512]{1,0:T(8,128)(2,1)S(1)}, bf16[144,512]{1,0:T(8,128)(2,1)S(1)}, u32[]{:S(2)}, u32[]{:S(2)}) collective-permute-start(bf16[144,512]{1,0:T(8,128)(2,1)S(1)} %copy-done.8), channel_id=1, source_target_pairs={{0,32},{32,64},{64,96},{96,128},{128,160},{160,192},{192,224},{224... | collective-permute-start | bytes 442376 | tf_op jit(solution)/shard_map/ppermute | solution.py:335
  128.9 4.1 %collective-permute-start.15 = (bf16[144,512]{1,0:T(8,128)(2,1)S(1)}, bf16[144,512]{1,0:T(8,128)(2,1)S(1)}, u32[]{:S(2)}, u32[]{:S(2)}) collective-permute-start(bf16[144,512]{1,0:T(8,128)(2,1)S(1)} %copy-done.10), channel_id=1, source_target_pairs={{0,8},{8,16},{16,24},{24,0},{1,9},{9,17},{17,25},{25,1},{2,10},{10... | collective-permute-start | bytes 442376 | tf_op jit(solution)/shard_map/ppermute | solution.py:335
  134.4 2.3 %collective-permute-done.12 = bf16[144,512]{1,0:T(8,128)(2,1)S(1)} collective-permute-done((bf16[144,512]{1,0:T(8,128)(2,1)S(1)}, bf16[144,512]{1,0:T(8,128)(2,1)S(1)}, u32[]{:S(2)}, u32[]{:S(2)}) %collective-permute-start.12) | collective-permute-done | bytes 147488 | tf_op jit(solution)/shard_map/ppermute | solution.py:333
  137.2 3.3 %collective-permute-done.14 = bf16[144,512]{1,0:T(8,128)(2,1)S(1)} collective-permute-done((bf16[144,512]{1,0:T(8,128)(2,1)S(1)}, bf16[144,512]{1,0:T(8,128)(2,1)S(1)}, u32[]{:S(2)}, u32[]{:S(2)}) %collective-permute-start.14) | collective-permute-done | bytes 147488 | tf_op jit(solution)/shard_map/ppermute | solution.py:335
  142.1 1.5 add_convert_fusion
  (120 shorter events, 13.7 us)
Async XLA Ops:
  7.2 61.3 %all-gather.2.cloned.1.call-start = ((), (), s32[]{:S(2)}) async-start(), calls=%async_computation | async-start | bytes 3538944 | tf_op jit(solution)/shard_map/all_gather | solution.py:359
  9.0 32.4 %collective-permute-start = (bf16[144,1024]{1,0:T(8,128)(2,1)S(1)}, bf16[144,1024]{1,0:T(8,128)(2,1)S(1)}, u32[]{:S(2)}, u32[]{:S(2)}) collective-permute-start(bf16[144,1024]{1,0:T(8,128)(2,1)S(1)} %reshape.78), channel_id=1, source_target_pairs={{0,24},{8,0},{16,8},{24,16},{1,25},{9,1},{17,9},{25,17},{2,26},{10... | collective-permute-start | bytes 884744 | tf_op jit(solution)/shard_map/ppermute | solution.py:335
  12.4 29.1 %collective-permute-start.1 = (bf16[144,1024]{1,0:T(8,128)(2,1)S(1)}, bf16[144,1024]{1,0:T(8,128)(2,1)S(1)}, u32[]{:S(2)}, u32[]{:S(2)}) collective-permute-start(bf16[144,1024]{1,0:T(8,128)(2,1)S(1)} %reshape.80), channel_id=1, source_target_pairs={{0,224},{32,0},{64,32},{96,64},{128,96},{160,128},{192,160},{224,1... | collective-permute-start | bytes 884744 | tf_op jit(solution)/shard_map/ppermute | solution.py:335
  15.9 25.6 %collective-permute-start.2 = (bf16[144,1024]{1,0:T(8,128)(2,1)S(1)}, bf16[144,1024]{1,0:T(8,128)(2,1)S(1)}, u32[]{:S(2)}, u32[]{:S(2)}) collective-permute-start(bf16[144,1024]{1,0:T(8,128)(2,1)S(1)} %reshape.82), channel_id=1, source_target_pairs={{0,248},{8,224},{16,232},{24,240},{32,24},{40,0},{48,8},{56,16},{6... | collective-permute-start | bytes 884744 | tf_op jit(solution)/shard_map/ppermute | solution.py:333
  52.7 14.6 %collective-permute-start.3 = (bf16[520,1024]{1,0:T(8,128)(2,1)}, bf16[520,1024]{1,0:T(8,128)(2,1)S(1)}, u32[]{:S(2)}, u32[]{:S(2)}) collective-permute-start(bf16[520,1024]{1,0:T(8,128)(2,1)} %get-tuple-element.60), channel_id=1, source_target_pairs={{0,8},{8,0},{16,24},{24,16},{1,9},{9,1},{17,25},{25,17},{2,10},{10... | collective-permute-start | bytes 3194888 | tf_op jit(solution)/shard_map/ppermute | solution.py:386
  68.5 22.4 %collective-permute-start.7 = (bf16[512,3072]{1,0:T(8,128)(2,1)}, bf16[512,3072]{1,0:T(8,128)(2,1)}, u32[]{:S(2)}, u32[]{:S(2)}) collective-permute-start(bf16[512,3072]{1,0:T(8,128)(2,1)} %all-gather.2.cloned.1.call-done.refs_6_), channel_id=1, source_target_pairs={{0,8},{8,0},{16,24},{24,16},{1,9},{9,1},{17,25},{25,17},{2,10},{10... | collective-permute-start | bytes 9437192 | tf_op jit(solution)/shard_map/ppermute | solution.py:384
  69.1 19.2 %collective-permute-start.4 = (bf16[136,1024]{1,0:T(8,128)(2,1)S(1)}, bf16[136,1024]{1,0:T(8,128)(2,1)S(1)}, u32[]{:S(2)}, u32[]{:S(2)}) collective-permute-start(bf16[136,1024]{1,0:T(8,128)(2,1)S(1)} %get-tuple-element.69), channel_id=1, source_target_pairs={{0,64},{8,24},{16,80},{24,40},{32,96},{40,56},{48,112},{56,8},{64,... | collective-permute-start | bytes 835592 | tf_op jit(solution)/shard_map/ppermute | solution.py:391
  69.5 18.8 %collective-permute-start.5 = (bf16[136,1024]{1,0:T(8,128)(2,1)S(1)}, bf16[136,1024]{1,0:T(8,128)(2,1)S(1)}, u32[]{:S(2)}, u32[]{:S(2)}) collective-permute-start(bf16[136,1024]{1,0:T(8,128)(2,1)S(1)} %get-tuple-element.70), channel_id=1, source_target_pairs={{0,128},{8,40},{16,144},{24,56},{32,160},{40,8},{48,176},{56,24},{... | collective-permute-start | bytes 835592 | tf_op jit(solution)/shard_map/ppermute | solution.py:391
  72.3 16.1 %collective-permute-start.6 = (bf16[136,1024]{1,0:T(8,128)(2,1)S(1)}, bf16[136,1024]{1,0:T(8,128)(2,1)S(1)}, u32[]{:S(2)}, u32[]{:S(2)}) collective-permute-start(bf16[136,1024]{1,0:T(8,128)(2,1)S(1)} %get-tuple-element.71), channel_id=1, source_target_pairs={{0,192},{8,56},{16,208},{24,8},{32,224},{40,24},{48,240},{56,40},{... | collective-permute-start | bytes 835592 | tf_op jit(solution)/shard_map/ppermute | solution.py:391
  88.8 7.5 %collective-permute-start.10 = (bf16[40,1024]{1,0:T(8,128)(2,1)S(1)}, bf16[40,1024]{1,0:T(8,128)(2,1)S(1)}, u32[]{:S(2)}, u32[]{:S(2)}) collective-permute-start(bf16[40,1024]{1,0:T(8,128)(2,1)S(1)} %get-tuple-element.89), channel_id=1, source_target_pairs={{0,32},{8,136},{16,48},{24,152},{32,0},{40,168},{48,16},{56,184},{... | collective-permute-start | bytes 245768 | tf_op jit(solution)/shard_map/ppermute | solution.py:391
  89.4 6.9 %collective-permute-start.11 = (bf16[40,1024]{1,0:T(8,128)(2,1)S(1)}, bf16[40,1024]{1,0:T(8,128)(2,1)S(1)}, u32[]{:S(2)}, u32[]{:S(2)}) collective-permute-start(bf16[40,1024]{1,0:T(8,128)(2,1)S(1)} %get-tuple-element.90), channel_id=1, source_target_pairs={{0,48},{8,200},{16,0},{24,216},{32,16},{40,232},{48,32},{56,248},{... | collective-permute-start | bytes 245768 | tf_op jit(solution)/shard_map/ppermute | solution.py:391
  96.7 20.2 %collective-permute-start.17 = (bf16[12,1024]{1,0:T(8,128)(2,1)S(1)}, bf16[12,1024]{1,0:T(8,128)(2,1)S(1)}, u32[]{:S(2)}, u32[]{:S(2)}) collective-permute-start(bf16[12,1024]{1,0:T(8,128)(2,1)S(1)} %get-tuple-element.124), channel_id=1, source_target_pairs={{0,1},{1,2},{2,3},{3,4},{4,5},{5,6},{6,7},{7,0},{8,9},{9,10},{10,1... | collective-permute-start | bytes 73736 | tf_op jit(solution)/shard_map/ppermute | solution.py:426
  98.7 20.7 %collective-permute-start.18 = (bf16[12,1024]{1,0:T(8,128)(2,1)S(1)}, bf16[12,1024]{1,0:T(8,128)(2,1)S(1)}, u32[]{:S(2)}, u32[]{:S(2)}) collective-permute-start(bf16[12,1024]{1,0:T(8,128)(2,1)S(1)} %get-tuple-element.125), channel_id=1, source_target_pairs={{0,2},{1,3},{2,4},{3,5},{4,6},{5,7},{6,0},{7,1},{8,10},{9,11},{10,... | collective-permute-start | bytes 73736 | tf_op jit(solution)/shard_map/ppermute | solution.py:426
  101.7 18.6 %collective-permute-start.19 = (bf16[12,1024]{1,0:T(8,128)(2,1)S(1)}, bf16[12,1024]{1,0:T(8,128)(2,1)S(1)}, u32[]{:S(2)}, u32[]{:S(2)}) collective-permute-start(bf16[12,1024]{1,0:T(8,128)(2,1)S(1)} %get-tuple-element.126), channel_id=1, source_target_pairs={{0,3},{1,4},{2,5},{3,6},{4,7},{5,0},{6,1},{7,2},{8,11},{9,12},{10,... | collective-permute-start | bytes 73736 | tf_op jit(solution)/shard_map/ppermute | solution.py:426
  105.4 19.8 %collective-permute-start.20 = (bf16[12,1024]{1,0:T(8,128)(2,1)S(1)}, bf16[12,1024]{1,0:T(8,128)(2,1)S(1)}, u32[]{:S(2)}, u32[]{:S(2)}) collective-permute-start(bf16[12,1024]{1,0:T(8,128)(2,1)S(1)} %get-tuple-element.127), channel_id=1, source_target_pairs={{0,4},{1,5},{2,6},{3,7},{4,0},{5,1},{6,2},{7,3},{8,12},{9,13},{10,... | collective-permute-start | bytes 73736 | tf_op jit(solution)/shard_map/ppermute | solution.py:426
  105.9 19.5 %collective-permute-start.21 = (bf16[12,1024]{1,0:T(8,128)(2,1)S(1)}, bf16[12,1024]{1,0:T(8,128)(2,1)S(1)}, u32[]{:S(2)}, u32[]{:S(2)}) collective-permute-start(bf16[12,1024]{1,0:T(8,128)(2,1)S(1)} %get-tuple-element.128), channel_id=1, source_target_pairs={{0,5},{1,6},{2,7},{3,0},{4,1},{5,2},{6,3},{7,4},{8,13},{9,14},{10,... | collective-permute-start | bytes 73736 | tf_op jit(solution)/shard_map/ppermute | solution.py:426
  117.0 9.2 %collective-permute-start.22 = (bf16[12,1024]{1,0:T(8,128)(2,1)S(1)}, bf16[12,1024]{1,0:T(8,128)(2,1)S(1)}, u32[]{:S(2)}, u32[]{:S(2)}) collective-permute-start(bf16[12,1024]{1,0:T(8,128)(2,1)S(1)} %get-tuple-element.129), channel_id=1, source_target_pairs={{0,6},{1,7},{2,0},{3,1},{4,2},{5,3},{6,4},{7,5},{8,14},{9,15},{10,... | collective-permute-start | bytes 73736 | tf_op jit(solution)/shard_map/ppermute | solution.py:426
  119.4 9.4 %collective-permute-start.23 = (bf16[12,1024]{1,0:T(8,128)(2,1)S(1)}, bf16[12,1024]{1,0:T(8,128)(2,1)S(1)}, u32[]{:S(2)}, u32[]{:S(2)}) collective-permute-start(bf16[12,1024]{1,0:T(8,128)(2,1)S(1)} %get-tuple-element.130), channel_id=1, source_target_pairs={{0,7},{1,0},{2,1},{3,2},{4,3},{5,4},{6,5},{7,6},{8,15},{9,8},{10,9... | collective-permute-start | bytes 73736 | tf_op jit(solution)/shard_map/ppermute | solution.py:426
  120.3 14.1 %collective-permute-start.8 = (bf16[144,512]{1,0:T(8,128)(2,1)S(1)}, bf16[144,512]{1,0:T(8,128)(2,1)S(1)}, u32[]{:S(2)}, u32[]{:S(2)}) collective-permute-start(bf16[144,512]{1,0:T(8,128)(2,1)S(1)} %copy-done.12), channel_id=1, source_target_pairs={{0,40},{8,48},{16,56},{24,32},{32,72},{40,80},{48,88},{56,64},{64,... | collective-permute-start | bytes 442376 | tf_op jit(solution)/shard_map/ppermute | solution.py:333
  125.2 11.5 %collective-permute-start.12 = (bf16[144,512]{1,0:T(8,128)(2,1)S(1)}, bf16[144,512]{1,0:T(8,128)(2,1)S(1)}, u32[]{:S(2)}, u32[]{:S(2)}) collective-permute-start(bf16[144,512]{1,0:T(8,128)(2,1)S(1)} %copy-done.9), channel_id=1, source_target_pairs={{0,40},{8,48},{16,56},{24,32},{32,72},{40,80},{48,88},{56,64},{64,... | collective-permute-start | bytes 442376 | tf_op jit(solution)/shard_map/ppermute | solution.py:333
  125.4 11.9 %collective-permute-start.13 = (bf16[144,512]{1,0:T(8,128)(2,1)S(1)}, bf16[144,512]{1,0:T(8,128)(2,1)S(1)}, u32[]{:S(2)}, u32[]{:S(2)}) collective-permute-start(bf16[144,512]{1,0:T(8,128)(2,1)S(1)} %copy-done.11), channel_id=1, source_target_pairs={{0,32},{32,64},{64,96},{96,128},{128,160},{160,192},{192,224},{224... | collective-permute-start | bytes 442376 | tf_op jit(solution)/shard_map/ppermute | solution.py:335
  126.2 14.4 %collective-permute-start.14 = (bf16[144,512]{1,0:T(8,128)(2,1)S(1)}, bf16[144,512]{1,0:T(8,128)(2,1)S(1)}, u32[]{:S(2)}, u32[]{:S(2)}) collective-permute-start(bf16[144,512]{1,0:T(8,128)(2,1)S(1)} %copy-done.8), channel_id=1, source_target_pairs={{0,32},{32,64},{64,96},{96,128},{128,160},{160,192},{192,224},{224... | collective-permute-start | bytes 442376 | tf_op jit(solution)/shard_map/ppermute | solution.py:335
  128.9 11.8 %collective-permute-start.15 = (bf16[144,512]{1,0:T(8,128)(2,1)S(1)}, bf16[144,512]{1,0:T(8,128)(2,1)S(1)}, u32[]{:S(2)}, u32[]{:S(2)}) collective-permute-start(bf16[144,512]{1,0:T(8,128)(2,1)S(1)} %copy-done.10), channel_id=1, source_target_pairs={{0,8},{8,16},{16,24},{24,0},{1,9},{9,17},{17,25},{25,1},{2,10},{10... | collective-permute-start | bytes 442376 | tf_op jit(solution)/shard_map/ppermute | solution.py:335
  134.4 6.3 %collective-permute-start.16 = (bf16[144,512]{1,0:T(8,128)(2,1)S(1)}, bf16[144,512]{1,0:T(8,128)(2,1)S(1)}, u32[]{:S(2)}, u32[]{:S(2)}) collective-permute-start(bf16[144,512]{1,0:T(8,128)(2,1)S(1)} %copy-done.7), channel_id=1, source_target_pairs={{0,8},{8,16},{16,24},{24,0},{1,9},{9,17},{17,25},{25,1},{2,10},{10... | collective-permute-start | bytes 442376 | tf_op jit(solution)/shard_map/ppermute | solution.py:335
  (14 other events, 116.5 us)
Sparse Core Ops, SparseCore 0:
  18.2 44.7 all-gather.1
where the time goes:
time: 151 us; the launch traced here: 150 us
  Pallas kernels  72.1 us (48%)
  starting transfers between devices  45 us (30%)
  between operations  14.7 us (10%)
  other arithmetic  7.35 us (5%)
  waiting for transfers between devices  6.09 us (4%)
  local copies, waits for them, and re-layouts  5.24 us (3%)
    pallas_call x2, Pallas kernels, backward(): pl.pallas_call(backward_kernel, grid=(count,), in_specs=[pl.BlockSpec((GR...  29.1 us
    pallas_call x1, Pallas kernels, forward(): pl.pallas_call(forward_kernel, grid=(count,), in_specs=[column_block(toke...  22.4 us
    ppermute x7, starting transfers between devices, per_device(): lax.ppermute(piece, 'dp', [(i, (i + n + 1) % d) for i in range(d)])  16.9 us
    ppermute x6, starting transfers between devices, shift(): lax.ppermute(value, name, [(i, (i + step) % count) for i in range(count)])  14.4 us
    pallas_call x2, Pallas kernels, back_product(): pl.pallas_call(back_kernel, grid=(steps,), in_specs=[pl.BlockSpec(memory_...  10.9 us
    pallas_call x1, Pallas kernels, middle(): pl.pallas_call(lambda *refs: middle_kernel(order, *refs), in_specs=[pl.Bl...  9.74 us
    ppermute x6, starting transfers between devices, plane_round(): lax.ppermute(piece, ('row', 'col'), plane_pairs(r, c, turn, n + 1))  6.81 us
    ppermute x3, starting transfers between devices, shift(): return lax.ppermute(value, ('row', 'col'), pairs)  6.31 us
  transfers between devices with their start and end apart: 25, of which 3 were waited for; matrix products, arithmetic and copies ran while one was open for 5% of the time, Pallas kernels for 48%

commit v1 on v0

--- a/solution.py
+++ b/solution.py
@@ -34,49 +34,103 @@
     return high, mid, (rest - mid.astype(F32)).astype(BF)
 
 
-def forward_kernel(q_ref, k_ref, v_ref, hot_ref, p_ref, o_ref, inv_ref):
+def by_head(parts):
+    return jnp.concatenate(parts, axis=0)
+
+
+def zero_unless(chosen, value):
+    return jnp.where(chosen, value, jnp.zeros_like(value))
+
+
+def forward_kernel(q_ref, k_ref, v_ref, hot_ref, p_ref, rest_ref, o_ref, inv_ref):
     tokens, lanes = q_ref.shape
     size = lanes // GROUP
+    main = p_ref.shape[2]
+    tail = tokens - main
     factor = size ** (-0.5) * math.log2(math.e)
     queries, keys, values, hot = q_ref[...], k_ref[...], v_ref[...], hot_ref[...]
     lane = lax.broadcasted_iota(jnp.int32, (tokens, lanes), 1)
     head = lane // size
     mask = jnp.where(lane % size < REGIONS, (hot.astype(F32) - 1.0) * 1e30, 0.0).astype(BF)
+    tail_keys, tail_values, tail_head = keys[main:], values[main:], head[:tail]
+    tail_mask = zero_unless(tail_head == 0, mask[main:])
+    tail_scores = lax.dot_general(
+        jnp.concatenate([queries, hot], axis=1),
+        jnp.concatenate(
+            [
+                by_head([zero_unless(tail_head == h, tail_keys) for h in range(GROUP)]),
+                by_head([tail_mask] * GROUP),
+            ],
+            axis=1,
+        ),
+        NT,
+        preferred_element_type=F32,
+    )
+    per = lanes // tail
+    main_head = head[:main]
 
     def scores_of(h):
-        left, right = jnp.where(head == h, queries, hot), jnp.where(head == h, keys, mask)
+        left = jnp.where(head == h, queries, hot)
+        right = jnp.where(main_head == h, keys[:main], mask[:main])
         return lax.dot_general(left, right, NT, preferred_element_type=F32)
 
-    def attend(h, expo):
-        summed = jnp.where(head == h, values, jnp.ones_like(values))
-        both = jnp.dot(expo, summed, preferred_element_type=F32)
-        inv = 1.0 / pltpu.roll(both, size, axis=1)
-        return both * inv, inv
-
     scores = scores_of(0)
-    last, out, inverse = None, None, None
+    last, sums, tops = None, [], []
     for h in range(GROUP + 1):
         ahead = scores_of(h + 1) if h + 1 < GROUP else None
         if last is not None:
-            attn, inv = attend(h - 1, last)
-            out = attn if out is None else jnp.where(head == h - 1, attn, out)
-            inverse = inv if inverse is None else jnp.where(head == h - 1, inv, inverse)
+            own = main_head == h - 1
+            summed = jnp.where(own, values[:main], jnp.ones_like(values[:main]))
+            sums.append(jnp.dot(last, summed, preferred_element_type=F32))
         if h < GROUP:
-            top = jnp.max(scores, axis=1, keepdims=True)
-            last = jnp.exp2((scores - top) * factor).astype(BF)
+            tile = tail_scores[:, lanes * (h // per) : lanes * (h // per + 1)]
+            top = jnp.where(lane // tail == h % per, tile, -3e38)
+            for start in range(0, main, lanes):
+                top = jnp.maximum(top, scores[:, start : start + lanes])
+            tops.append(jnp.max(top, axis=1, keepdims=True))
+            last = jnp.exp2((scores - tops[h]) * factor).astype(BF)
             p_ref[h] = last
         scores = ahead
-    o_ref[...] = out
+    rest = []
+    for n in range(GROUP // per):
+        top = tops[n * per]
+        for i in range(1, per):
+            top = jnp.where(lane // tail == i, tops[n * per + i], top)
+        tile = tail_scores[:, lanes * n : lanes * (n + 1)]
+        rest.append(jnp.exp2((tile - top) * factor).astype(BF))
+    rest = jnp.concatenate(rest, axis=1)
+    rest_ref[...] = rest
+    ones = jnp.ones_like(tail_values)
+    right = by_head(
+        [
+            jnp.concatenate(
+                [zero_unless(tail_head == h, tail_values), zero_unless(tail_head == h, ones)], axis=1
+            )
+            for h in range(GROUP)
+        ]
+    )
+    both = jnp.dot(rest, right, preferred_element_type=F32)
+    out, total = None, None
+    for h, part in enumerate(sums):
+        turned = pltpu.roll(part, size, axis=1)
+        out = part if out is None else jnp.where(head == h, part, out)
+        total = turned if total is None else jnp.where(head == h, turned, total)
+    inverse = 1.0 / (total + both[:, lanes:])
+    o_ref[...] = (out + both[:, :lanes]) * inverse
     inv_ref[...] = inverse
 
 
-def backward_kernel(p_ref, q_ref, k_ref, v_ref, do_ref, o_ref, inv_ref, dq_ref, dk_ref, dv_ref):
+def backward_kernel(
+    p_ref, rest_ref, q_ref, k_ref, v_ref, do_ref, o_ref, inv_ref, dq_ref, dk_ref, dv_ref
+):
     tokens, lanes = q_ref.shape
     size = lanes // GROUP
+    main = p_ref.shape[2]
+    tail = tokens - main
     scale = size ** (-0.5)
     keys, values, dout, inv = k_ref[...], v_ref[...], do_ref[...], inv_ref[...]
     lane = lax.broadcasted_iota(jnp.int32, (tokens, lanes), 1)
-    head = lane // size
+    head, which = lane // size, lane % size
     dout_f = dout.astype(F32)
     row_i = lax.broadcasted_iota(jnp.int32, (lanes, lanes), 0) // size
     col_i = lax.broadcasted_iota(jnp.int32, (lanes, lanes), 1)
@@ -86,16 +140,32 @@
     d_high = delta.astype(BF).astype(F32)
     d_rest = delta - d_high
     d_mid = d_rest.astype(BF).astype(F32)
-    which = lane % size
     columns = jnp.where(
         which == 0, d_high, jnp.where(which == 1, d_mid, jnp.where(which == 2, d_rest - d_mid, 0.0))
     ).astype(BF)
     dout_t = (dout_f * inv).T.astype(BF)
     query_t = (q_ref[...].astype(F32) * (inv * scale)).T.astype(BF)
+    tail_head, main_head = head[:tail], head[:main]
+
+    def minus(h, count):
+        chosen = (head[:count] == (h + 1) % GROUP) & (which[:count] < 3)
+        return jnp.where(chosen, -1.0, 0.0).astype(BF)
+
+    rest = rest_ref[...]
+    right = by_head(
+        [
+            jnp.concatenate([zero_unless(tail_head == h, values[main:]), minus(h, tail)], axis=1)
+            for h in range(GROUP)
+        ]
+    )
+    dprobs = lax.dot_general(
+        jnp.concatenate([dout, columns], axis=1), right, NT, preferred_element_type=F32
+    )
+    dscores_rest = (rest.astype(F32) * dprobs).astype(BF)
 
     def dprobs_of(h):
-        minus = jnp.where((head == (h + 1) % GROUP) & (which < 3), -1.0, 0.0).astype(BF)
-        left, right = jnp.where(head == h, dout, columns), jnp.where(head == h, values, minus)
+        left = jnp.where(head == h, dout, columns)
+        right = jnp.where(main_head == h, values[:main], minus(h, main))
         return lax.dot_general(left, right, NT, preferred_element_type=F32)
 
     dprobs = dprobs_of(0)
@@ -104,48 +174,71 @@
         ahead = dprobs_of(h + 1) if h + 1 < GROUP else None
         probs = p_ref[h]
         dscores = (probs.astype(F32) * dprobs).astype(BF)
-        part = jnp.dot(dscores, keys, preferred_element_type=F32)
+        part = jnp.dot(dscores, keys[:main], preferred_element_type=F32)
         dq = part if dq is None else jnp.where(head == h, part, dq)
         rows = slice(size * h, size * (h + 1))
         dks.append(jnp.dot(query_t[rows], dscores, preferred_element_type=F32))
         dvs.append(jnp.dot(dout_t[rows], probs, preferred_element_type=F32))
         dprobs = ahead
+    right = by_head([zero_unless(tail_head == h, keys[main:]) for h in range(GROUP)])
+    dq = dq + jnp.dot(dscores_rest, right, preferred_element_type=F32)
     dq_ref[...] = (dq * (inv * scale)).astype(BF)
-    dk_ref[...] = jnp.concatenate(dks, axis=0).T.astype(BF)
-    dv_ref[...] = jnp.concatenate(dvs, axis=0).T.astype(BF)
+    for ref, whole, left, right in (
+        (dk_ref, dks, query_t, dscores_rest),
+        (dv_ref, dvs, dout_t, rest),
+    ):
+        ref[0:main] = jnp.concatenate(whole, axis=0).T.astype(BF)
+        turned = jnp.dot(left, right, preferred_element_type=F32).T
+        last = turned[0:tail]
+        for h in range(1, GROUP):
+            last = jnp.where(tail_head == h, turned[tail * h : tail * (h + 1)], last)
+        ref[main:] = last.astype(BF)
 
 
 def column_block(tokens, offset):
     return pl.BlockSpec((tokens, 128), lambda g: (0, g + offset))
 
 
-def forward(qkv, hot, first, count):
+def forward(qkv, hot):
     tokens = qkv.shape[0]
     per = qkv.shape[1] // 3 // 128
-    whole = pl.BlockSpec((tokens, 128), lambda g: (0, 0))
-    out = shape(tokens, count * 128)(F32)
+    main = tokens // 256 * 256
+    rest = (tokens - main) * GROUP
+    out = shape(tokens, per * 128)(F32)
     return pl.pallas_call(
         forward_kernel,
-        grid=(count,),
-        in_specs=[column_block(tokens, first + per * i) for i in range(3)] + [whole],
-        out_specs=[pl.BlockSpec((GROUP, tokens, tokens), lambda g: (g, 0, 0))]
+        grid=(per,),
+        in_specs=[column_block(tokens, per * i) for i in range(3)]
+        + [pl.BlockSpec((tokens, 128), lambda g: (0, 0))],
+        out_specs=[
+            pl.BlockSpec((GROUP, tokens, main), lambda g: (g, 0, 0)),
+            pl.BlockSpec((tokens, rest), lambda g: (0, g)),
+        ]
         + [column_block(tokens, 0)] * 2,
-        out_shape=[shape(count * GROUP, tokens, tokens)(BF), out, out],
+        out_shape=[
+            shape(per * GROUP, tokens, main)(BF),
+            shape(tokens, per * rest)(BF),
+            out,
+            out,
+        ],
         compiler_params=params(),
         cost_estimate=pl.CostEstimate(
-            flops=count * 3_200_000_000, bytes_accessed=count * 4_000_000, transcendentals=0
+            flops=per * 3_200_000_000, bytes_accessed=per * 4_000_000, transcendentals=0
         ),
         name="attn_forward",
     )(qkv, qkv, qkv, hot)
 
 
-def backward(probs, qkv, dattn, out, inverse, first, count):
+def backward(probs, rest, qkv, dattn, out, inverse, first, count):
     tokens = qkv.shape[0]
     per = qkv.shape[1] // 3 // 128
     return pl.pallas_call(
         backward_kernel,
         grid=(count,),
-        in_specs=[pl.BlockSpec((GROUP, tokens, tokens), lambda g: (g + first, 0, 0))]
+        in_specs=[
+            pl.BlockSpec((GROUP, *probs.shape[1:]), lambda g: (g + first, 0, 0)),
+            pl.BlockSpec((tokens, rest.shape[1] // per), lambda g: (0, g + first)),
+        ]
         + [column_block(tokens, first + per * i) for i in range(3)]
         + [column_block(tokens, first)] * 3,
         out_specs=[column_block(tokens, 0)] * 3,
@@ -155,7 +248,7 @@
             flops=count * 3_600_000_000, bytes_accessed=count * 4_000_000, transcendentals=0
         ),
         name="attn_backward",
-    )(probs, qkv, qkv, qkv, dattn, out, inverse)
+    )(probs, rest, qkv, qkv, qkv, dattn, out, inverse)
 
 
 def pack_gain(high, low):
@@ -218,7 +311,7 @@
 
 
 def back_kernel(core_ref, *refs):
-    parts, (mine_ref, other_ref), outs = refs[:6], refs[6:8], refs[8:]
+    parts, (mine_ref, other_ref), outs = refs[:-6], refs[-6:-4], refs[-4:]
     first = core_ref[0] == 0
     left = jnp.concatenate([ref[...] for ref in parts], axis=1)
     rows = 64
@@ -236,12 +329,12 @@
         ).astype(BF)
 
 
-def back_product(parts, mine, other, core, which):
+def back_product(parts, mine, other, core):
     tokens = parts[0].shape[0]
     rows, inner = mine.shape
-    steps = 2
-    wide = 2 * rows // (2 * steps)
-    side = pl.BlockSpec((rows // (2 * steps), inner), lambda g: (g + which * steps, 0))
+    steps = 4
+    wide = 2 * rows // steps
+    side = pl.BlockSpec((rows // steps, inner), lambda g: (g, 0))
     out = pl.BlockSpec((tokens // 4, wide), lambda g: (0, g))
     return pl.pallas_call(
         back_kernel,
@@ -253,7 +346,7 @@
         out_shape=[shape(tokens // 4, wide * steps)(BF)] * 4,
         compiler_params=params(),
         cost_estimate=pl.CostEstimate(
-            flops=2_500_000_000, bytes_accessed=8_000_000, transcendentals=0
+            flops=6_000_000_000, bytes_accessed=12_000_000, transcendentals=0
         ),
         name="back_product",
     )(core, *parts, mine, other)
@@ -316,6 +409,8 @@
     for value in got:
         own = own + value[GAIN_ROWS:].astype(F32)
         gains.append(value[0:1].astype(F32) + value[1:2].astype(F32))
+    if count == 2:
+        return own, gains[0] + gains[1]
     turned = jnp.concatenate(gains[::-1] * 2, axis=0)
     ordered = lax.dynamic_slice_in_dim(turned, count - 1 - index, count, 0)
     gain = ordered[0:1]
@@ -367,7 +462,7 @@
     qkv_t = qkv.reshape(tokens, 3 * width)
     groups = width // 128
     qkv_t, mine_w = lax.optimization_barrier((qkv_t, mine_w))
-    probs, out, inverse = forward(qkv_t, hot, 0, groups)
+    probs, rest, out, inverse = forward(qkv_t, hot)
 
     dz = jnp.concatenate(
         [
@@ -392,9 +487,20 @@
             for n, piece in enumerate(pieces)
         ]
 
-    half_groups = groups // 2
-    early = backward(probs, qkv_t, dattn, out, inverse, 0, half_groups)
-    early, got = lax.optimization_barrier((early, got))
+    def back_part(dattn, first, count):
+        return backward(probs, rest, qkv_t, dattn, out, inverse, first, count)
+
+    def halve(sums, gain, bit):
+        index = dp // bit % 2
+        (piece,), own, gain = round_pieces(sums, gain, index, 2)
+        return piece, own, gain, index
+
+    def swap(piece, bit):
+        return lax.ppermute(piece, "dp", [(i, i ^ bit) for i in range(d)])
+
+    first, second = groups // 4, groups // 4 + (groups - groups // 4) // 2
+    part_a = back_part(dattn, 0, first)
+    part_a, got = lax.optimization_barrier((part_a, got))
     sums = keep + got[GAIN_ROWS:].astype(F32)
     gain = gain + (got[0:1].astype(F32) + got[1:2].astype(F32))
     index = jnp.where(core == 0, x, y)
@@ -402,35 +508,37 @@
     dattn, pieces = lax.optimization_barrier((dattn, pieces))
     got = plane_round(pieces, 0)
 
-    late = backward(probs, qkv_t, dattn, out, inverse, half_groups, half_groups)
-    late, got = lax.optimization_barrier((late, got))
+    part_b = back_part(dattn, first, second - first)
+    part_b, got = lax.optimization_barrier((part_b, got))
     sums, gain = round_sums(got, own, gain, index)
     index = jnp.where(core == 0, y, x)
     pieces, own, gain = round_pieces(sums, gain, index, RADIX)
-    late, pieces = lax.optimization_barrier((late, pieces))
+    dattn, pieces = lax.optimization_barrier((dattn, pieces))
     got = plane_round(pieces, 1)
 
-    parts = [part for pair in zip(early, late) for part in pair]
-    moved = []
-    for n in range(2):
-        quarters = back_product(parts, mine, other, bit, n)
-        if n == 1:
-            quarters, got = lax.optimization_barrier((quarters, got))
-        moved.append(
-            [quarters[0]] + [shift(quarters[i], i // 2 == 1, i % 2 == 1, 1) for i in (1, 2, 3)]
-        )
-
+    part_c = back_part(dattn, second, groups - second)
+    part_c, got = lax.optimization_barrier((part_c, got))
     sums, gain = round_sums(got, own, gain, index)
-    pieces, own, gain = round_pieces(sums, gain, dp, d)
-    got = [
-        lax.ppermute(piece, "dp", [(i, (i + n + 1) % d) for i in range(d)])
-        for n, piece in enumerate(pieces)
+    piece, own, gain, index = halve(sums, gain, 4)
+    part_c, piece = lax.optimization_barrier((part_c, piece))
+    got = swap(piece, 4)
+
+    parts = [part for trio in zip(part_a, part_b, part_c) for part in trio]
+    quarters = back_product(parts, mine, other, bit)
+    quarters, got = lax.optimization_barrier((quarters, got))
+    local, to_col, to_row, to_both = [quarters[0]] + [
+        shift(quarters[i], i // 2 == 1, i % 2 == 1, 1) for i in (1, 2, 3)
     ]
-    sums, gain = round_sums(got, own, gain, dp)
+    sums, gain = round_sums([got], own, gain, index)
+    piece, own, gain, index = halve(sums, gain, 2)
+    sums, gain = round_sums([swap(piece, 2)], own, gain, index)
+    sums, to_col = lax.optimization_barrier((sums, to_col))
+    piece, own, gain, index = halve(sums, gain, 1)
+    sums, gain = round_sums([swap(piece, 1)], own, gain, index)
     grad_proj, grad_gain = sums * norm, gain * norm
 
     local, to_col, to_row, to_both = (
-        jnp.concatenate(pair, axis=1).reshape(square) for pair in zip(*moved)
+        part.reshape(square) for part in (local, to_col, to_row, to_both)
     )
     moved = jnp.concatenate(
         [

time: 151 us -> 136 us (0.901)
  starting transfers between devices: 45 us -> 29.4 us
  waiting for transfers between devices: 6.09 us -> 12.8 us
  Pallas kernels: 72.1 us -> 68 us
    ppermute x7 -> x3, starting transfers between devices: 16.9 us -> 9.16 us  [swap(): return lax.ppermute(piece, 'dp', [(i, i ^ bit) for i in range(d)])]
    ppermute x3 -> x2, waiting for transfers between devices: 2.3 us -> 8.07 us  [shift(): return lax.ppermute(value, ('row', 'col'), pairs)]
    ppermute x6 -> x4, starting transfers between devices: 14.4 us -> 9.23 us  [shift(): lax.ppermute(value, name, [(i, (i + step) % count) for i in range(count)])]
    ppermute x3 -> x2, starting transfers between devices: 6.31 us -> 2.29 us  [shift(): return lax.ppermute(value, ('row', 'col'), pairs)]
    pallas_call x2 -> x1, Pallas kernels: 10.9 us -> 8.03 us  [back_product(): pl.pallas_call(back_kernel, grid=(steps,), in_specs=[pl.BlockSpec(memory_...]
    pallas_call x1, Pallas kernels: 22.4 us -> 20.3 us  [forward(): pl.pallas_call(forward_kernel, grid=(per,), in_specs=[column_block(tokens...]
    ppermute x6, starting transfers between devices: 6.81 us -> 8.56 us  [plane_round(): lax.ppermute(piece, ('row', 'col'), plane_pairs(r, c, turn, n + 1))]
    pallas_call x2 -> x3, Pallas kernels: 29.1 us -> 30.1 us  [backward(): pl.pallas_call(backward_kernel, grid=(count,), in_specs=[pl.BlockSpec((GR...]
  transfers between devices with their start and end apart: 25 -> 18, of which waited for: 3 -> 3; matrix products, arithmetic and copies ran while one was open for 5% -> 6% of each run, Pallas kernels for 48% -> 50%
where the time goes in v1:
time: 136 us
  Pallas kernels  68 us (50%)
  starting transfers between devices  29.4 us (22%)
  between operations  14.5 us (11%)
  waiting for transfers between devices  12.8 us (9%)
  other arithmetic  6.38 us (5%)
  local copies, waits for them, and re-layouts  4.88 us (4%)
    pallas_call x3, Pallas kernels, backward(): pl.pallas_call(backward_kernel, grid=(count,), in_specs=[pl.BlockSpec((GR...  30.1 us
    pallas_call x1, Pallas kernels, forward(): pl.pallas_call(forward_kernel, grid=(per,), in_specs=[column_block(tokens...  20.3 us
    pallas_call x1, Pallas kernels, middle(): pl.pallas_call(lambda *refs: middle_kernel(order, *refs), in_specs=[pl.Bl...  9.69 us
    ppermute x4, starting transfers between devices, shift(): lax.ppermute(value, name, [(i, (i + step) % count) for i in range(count)])  9.23 us
    ppermute x3, starting transfers between devices, swap(): return lax.ppermute(piece, 'dp', [(i, i ^ bit) for i in range(d)])  9.16 us
    ppermute x6, starting transfers between devices, plane_round(): lax.ppermute(piece, ('row', 'col'), plane_pairs(r, c, turn, n + 1))  8.56 us
    ppermute x2, waiting for transfers between devices, shift(): return lax.ppermute(value, ('row', 'col'), pairs)  8.07 us
    pallas_call x1, Pallas kernels, back_product(): pl.pallas_call(back_kernel, grid=(steps,), in_specs=[pl.BlockSpec(memory_...  8.03 us
  transfers between devices with their start and end apart: 18, of which 3 were waited for; matrix products, arithmetic and copies ran while one was open for 6% of the time, Pallas kernels for 50%

profile of v1, /device:TPU:1, one launch (start us, length us, event | category | flops | bytes accessed | tf_op | source)
XLA Modules:
  0.0 136.0 jit_solution(8394911198448480967)
XLA Ops:
  7.2 1.7 %fusion.18 = (bf16[12,12,1024]{2,1,0:T(8,128)(2,1)S(1)}, bf16[12,12,1024]{2,1,0:T(8,128)(2,1)S(1)}, bf16[12,12,1024]{2,1,0:T(8,128)(2,1)S(1)}, bf16[12,12,1024]{2,1,0:T(8,128)(2,1)S(1)}) fusion(bf16[24,24,1024]{2,1,0:T(8,128)(2,1)} %bitcast.32), kind=kLoop, calls=%fused_computation.82 | loop fusion | bytes 2359296 | tf_op jit(solution)/shard_map/slice | solution.py:437
  9.0 3.3 %collective-permute-start = (bf16[144,1024]{1,0:T(8,128)(2,1)S(1)}, bf16[144,1024]{1,0:T(8,128)(2,1)S(1)}, u32[]{:S(2)}, u32[]{:S(2)}) collective-permute-start(bf16[144,1024]{1,0:T(8,128)(2,1)S(1)} %reshape.78), channel_id=1, source_target_pairs={{0,24},{8,0},{16,8},{24,16},{1,25},{9,1},{17,9},{25,17},{2,26},{10... | collective-permute-start | bytes 884744 | tf_op jit(solution)/shard_map/ppermute | solution.py:430
  12.4 3.5 %collective-permute-start.1 = (bf16[144,1024]{1,0:T(8,128)(2,1)S(1)}, bf16[144,1024]{1,0:T(8,128)(2,1)S(1)}, u32[]{:S(2)}, u32[]{:S(2)}) collective-permute-start(bf16[144,1024]{1,0:T(8,128)(2,1)S(1)} %reshape.80), channel_id=1, source_target_pairs={{0,224},{32,0},{64,32},{96,64},{128,96},{160,128},{192,160},{224,1... | collective-permute-start | bytes 884744 | tf_op jit(solution)/shard_map/ppermute | solution.py:430
  16.0 1.3 collective-permute-start.2
  19.1 20.3 %attn_forward.1 = (bf16[32,576,512]{2,1,0:T(8,128)(2,1)}, bf16[576,2048]{1,0:T(8,128)(2,1)}, f32[576,1024]{1,0:T(8,128)}, f32[576,1024]{1,0:T(8,128)}) custom-call(bf16[576,3072]{1,0:T(8,128)(2,1)} %bitcast.20, bf16[576,3072]{1,0:T(8,128)(2,1)} %bitcast.21, bf16[576,3072]{1,0:T(8,128)(2,1)} %bitcast.22, bf16[576,128]{1,0:T(8,128)(2,1)} %fusion.hot_ref), custom_call_target="tpu_custom_call" | custom-call | flops 25600000000 | bytes 32000000 | tf_op jit(solution)/shard_map/attn_forward/pallas_call | solution.py:208
  39.6 1.4 maximum_maximum_fusion
  40.9 9.7 %middle.1 = (bf16[576,1024]{1,0:T(8,128)(2,1)}, bf16[520,1024]{1,0:T(8,128)(2,1)}, f32[512,1024]{1,0:T(8,128)}, f32[1,1024]{1,0:T(1,128)}) custom-call(s32[1]{0:T(128)} %bitcast.refs_0_.core_ref, f32[576,1024]{1,0:T(8,128)} %get-tuple-element.63.refs_1_.o_ref, bf16[1024,1024]{1,0:T(8,128)(2,1)} %refs_2_.1, bf16[576,1024]{1,0:T(8,128)(2,1)} %bitcast.33, ...), custom_call_target="tpu_custom_call" | custom-call | flops 8000000000 | bytes 16000000 | tf_op jit(solution)/shard_map/middle/pallas_call | solution.py:294
  50.6 8.3 %attn_backward.3 = (bf16[576,256]{1,0:T(8,128)(2,1)}, bf16[576,256]{1,0:T(8,128)(2,1)}, bf16[576,256]{1,0:T(8,128)(2,1)}) custom-call(bf16[32,576,512]{2,1,0:T(8,128)(2,1)} %get-tuple-element.61.p_ref, bf16[576,2048]{1,0:T(8,128)(2,1)} %get-tuple-element.62.rest_ref, bf16[576,3072]{1,0:T(8,128)(2,1)} %bitcast.23, bf16[576,3072]{1,0:T(8,128)(2,1)} %bitcast.24, ...), custom_call_target="tpu_custom_call" | custom-call | flops 7200000000 | bytes 8000000 | tf_op jit(solution)/shard_map/attn_backward/pallas_call | solution.py:235
  60.2 2.8 %collective-permute-start.5 = (bf16[136,1024]{1,0:T(8,128)(2,1)S(1)}, bf16[136,1024]{1,0:T(8,128)(2,1)S(1)}, u32[]{:S(2)}, u32[]{:S(2)}) collective-permute-start(bf16[136,1024]{1,0:T(8,128)(2,1)S(1)} %get-tuple-element.79), channel_id=1, source_target_pairs={{0,128},{8,40},{16,144},{24,56},{32,160},{40,8},{48,176},{56,24},{... | collective-permute-start | bytes 835592 | tf_op jit(solution)/shard_map/ppermute | solution.py:486
  63.0 1.6 %collective-permute-start.6 = (bf16[136,1024]{1,0:T(8,128)(2,1)S(1)}, bf16[136,1024]{1,0:T(8,128)(2,1)S(1)}, u32[]{:S(2)}, u32[]{:S(2)}) collective-permute-start(bf16[136,1024]{1,0:T(8,128)(2,1)S(1)} %get-tuple-element.80), channel_id=1, source_target_pairs={{0,192},{8,56},{16,208},{24,8},{32,224},{40,24},{48,240},{56,40},{... | collective-permute-start | bytes 835592 | tf_op jit(solution)/shard_map/ppermute | solution.py:486
  64.6 10.9 %attn_backward.4 = (bf16[576,384]{1,0:T(8,128)(2,1)}, bf16[576,384]{1,0:T(8,128)(2,1)}, bf16[576,384]{1,0:T(8,128)(2,1)}) custom-call(bf16[32,576,512]{2,1,0:T(8,128)(2,1)} %get-tuple-element.61.p_ref, bf16[576,2048]{1,0:T(8,128)(2,1)} %get-tuple-element.62.rest_ref, bf16[576,3072]{1,0:T(8,128)(2,1)} %bitcast.26, bf16[576,3072]{1,0:T(8,128)(2,1)} %bitcast.27, ...), custom_call_target="tpu_custom_call" | custom-call | flops 10800000000 | bytes 12000000 | tf_op jit(solution)/shard_map/attn_backward/pallas_call | solution.py:235
  76.2 1.7 %collective-permute-start.8 = (bf16[40,1024]{1,0:T(8,128)(2,1)S(1)}, bf16[40,1024]{1,0:T(8,128)(2,1)S(1)}, u32[]{:S(2)}, u32[]{:S(2)}) collective-permute-start(bf16[40,1024]{1,0:T(8,128)(2,1)S(1)} %get-tuple-element.90), channel_id=1, source_target_pairs={{0,32},{8,136},{16,48},{24,152},{32,0},{40,168},{48,16},{56,184},{... | collective-permute-start | bytes 245768 | tf_op jit(solution)/shard_map/ppermute | solution.py:486
  77.9 2.0 %collective-permute-start.9 = (bf16[40,1024]{1,0:T(8,128)(2,1)S(1)}, bf16[40,1024]{1,0:T(8,128)(2,1)S(1)}, u32[]{:S(2)}, u32[]{:S(2)}) collective-permute-start(bf16[40,1024]{1,0:T(8,128)(2,1)S(1)} %get-tuple-element.91), channel_id=1, source_target_pairs={{0,48},{8,200},{16,0},{24,216},{32,16},{40,232},{48,32},{56,248},{... | collective-permute-start | bytes 245768 | tf_op jit(solution)/shard_map/ppermute | solution.py:486
  79.9 10.9 %attn_backward.5 = (bf16[576,384]{1,0:T(8,128)(2,1)}, bf16[576,384]{1,0:T(8,128)(2,1)}, bf16[576,384]{1,0:T(8,128)(2,1)}) custom-call(bf16[32,576,512]{2,1,0:T(8,128)(2,1)} %get-tuple-element.61.p_ref, bf16[576,2048]{1,0:T(8,128)(2,1)} %get-tuple-element.62.rest_ref, bf16[576,3072]{1,0:T(8,128)(2,1)} %bitcast.29, bf16[576,3072]{1,0:T(8,128)(2,1)} %bitcast.30, ...), custom_call_target="tpu_custom_call" | custom-call | flops 10800000000 | bytes 12000000 | tf_op jit(solution)/shard_map/attn_backward/pallas_call | solution.py:235
  91.1 7.0 %collective-permute-start.11 = (bf16[24,1024]{1,0:T(8,128)(2,1)S(1)}, bf16[24,1024]{1,0:T(8,128)(2,1)S(1)}, u32[]{:S(2)}, u32[]{:S(2)}) collective-permute-start(bf16[24,1024]{1,0:T(8,128)(2,1)S(1)} %pad_maximum_fusion.6), channel_id=1, source_target_pairs={{0,4},{1,5},{2,6},{3,7},{4,0},{5,1},{6,2},{7,3},{8,12},{9,13},{10,... | collective-permute-start | bytes 147464 | tf_op jit(solution)/shard_map/ppermute | solution.py:499
  98.1 8.0 %back_product.1 = (bf16[144,1024]{1,0:T(8,128)(2,1)}, bf16[144,1024]{1,0:T(8,128)(2,1)}, bf16[144,1024]{1,0:T(8,128)(2,1)}, bf16[144,1024]{1,0:T(8,128)(2,1)}) custom-call(s32[1]{0:T(128)} %bitcast.refs_0_.core_ref, bf16[576,256]{1,0:T(8,128)(2,1)} %get-tuple-element.70.refs_0_, bf16[576,384]{1,0:T(8,128)(2,1)} %get-tuple-element.81.refs_1_, ...), custom_call_target="tpu_custom_call" | custom-call | flops 6000000000 | bytes 12000000 | tf_op jit(solution)/shard_map/back_product/pallas_call | solution.py:339
  106.3 1.3 collective-permute-start.14
  107.6 1.3 collective-permute-start.15
  109.9 1.1 collective-permute-start.13
  111.0 1.0 reshape.88
  112.2 1.9 %collective-permute-done.15 = bf16[144,1024]{1,0:T(8,128)(2,1)S(1)} collective-permute-done((bf16[144,1024]{1,0:T(8,128)(2,1)}, bf16[144,1024]{1,0:T(8,128)(2,1)S(1)}, u32[]{:S(2)}, u32[]{:S(2)}) %collective-permute-start.15) | collective-permute-done | bytes 294944 | tf_op jit(solution)/shard_map/ppermute | solution.py:430
  115.1 8.1 %collective-permute-done.12 = bf16[144,1024]{1,0:T(8,128)(2,1)S(1)} collective-permute-done((bf16[144,1024]{1,0:T(8,128)(2,1)}, bf16[144,1024]{1,0:T(8,128)(2,1)S(1)}, u32[]{:S(2)}, u32[]{:S(2)}) %collective-permute-start.12) | collective-permute-done | bytes 294944 | tf_op jit(solution)/shard_map/ppermute | solution.py:428
  123.2 2.8 %collective-permute-done.13 = bf16[144,1024]{1,0:T(8,128)(2,1)S(1)} collective-permute-done((bf16[144,1024]{1,0:T(8,128)(2,1)}, bf16[144,1024]{1,0:T(8,128)(2,1)S(1)}, u32[]{:S(2)}, u32[]{:S(2)}) %collective-permute-start.13) | collective-permute-done | bytes 294944 | tf_op jit(solution)/shard_map/ppermute | solution.py:430
  126.5 1.5 %add_convert_fusion = bf16[1,24,24,1024]{3,2,1,0:T(8,128)(2,1)} fusion(bf16[1,24,24,1024]{3,2,1,0:T(8,128)(2,1)S(1)} %copy-done.2, bf16[1,12,24,1024]{3,2,1,0:T(8,128)(2,1)S(1)} %maximum_bitcast_fusion.1, bf16[1,12,24,1024]{3,2,1,0:T(8,128)(2,1)S(1)} %maximum_bitcast_fusion), kind=kLoop, calls=%fused_computation | loop fusion | flops 2949120 | bytes 3538944 | tf_op jit(solution)/shard_map/convert_element_type | solution.py:550
  (92 shorter events, 8.2 us)
Async XLA Ops:
  7.2 10.1 %copy-start = (bf16[128,3072]{1,0:T(8,128)(2,1)S(1)}, bf16[128,3072]{1,0:T(8,128)(2,1)}, u32[]{:S(2)}) copy-start(bf16[128,3072]{1,0:T(8,128)(2,1)} %param.8) | copy-start | bytes 2359300
  7.2 68.7 %all-gather.2.cloned.1.call-start = ((), (), s32[]{:S(2)}) async-start(), calls=%async_computation | async-start | bytes 3538944 | tf_op jit(solution)/shard_map/all_gather | solution.py:454
  9.0 9.2 %copy-start.4 = (s32[24,24]{1,0:T(8,128)S(1)}, s32[24,24]{1,0:T(8,128)}, u32[]{:S(2)}) copy-start(s32[24,24]{1,0:T(8,128)} %param.11) | copy-start | bytes 6916
  9.0 30.3 %collective-permute-start = (bf16[144,1024]{1,0:T(8,128)(2,1)S(1)}, bf16[144,1024]{1,0:T(8,128)(2,1)S(1)}, u32[]{:S(2)}, u32[]{:S(2)}) collective-permute-start(bf16[144,1024]{1,0:T(8,128)(2,1)S(1)} %reshape.78), channel_id=1, source_target_pairs={{0,24},{8,0},{16,8},{24,16},{1,25},{9,1},{17,9},{25,17},{2,26},{10... | collective-permute-start | bytes 884744 | tf_op jit(solution)/shard_map/ppermute | solution.py:430
  12.4 27.0 %collective-permute-start.1 = (bf16[144,1024]{1,0:T(8,128)(2,1)S(1)}, bf16[144,1024]{1,0:T(8,128)(2,1)S(1)}, u32[]{:S(2)}, u32[]{:S(2)}) collective-permute-start(bf16[144,1024]{1,0:T(8,128)(2,1)S(1)} %reshape.80), channel_id=1, source_target_pairs={{0,224},{32,0},{64,32},{96,64},{128,96},{160,128},{192,160},{224,1... | collective-permute-start | bytes 884744 | tf_op jit(solution)/shard_map/ppermute | solution.py:430
  16.0 23.5 %collective-permute-start.2 = (bf16[144,1024]{1,0:T(8,128)(2,1)S(1)}, bf16[144,1024]{1,0:T(8,128)(2,1)S(1)}, u32[]{:S(2)}, u32[]{:S(2)}) collective-permute-start(bf16[144,1024]{1,0:T(8,128)(2,1)S(1)} %reshape.82), channel_id=1, source_target_pairs={{0,248},{8,224},{16,232},{24,240},{32,24},{40,0},{48,8},{56,16},{6... | collective-permute-start | bytes 884744 | tf_op jit(solution)/shard_map/ppermute | solution.py:428
  50.6 8.4 %collective-permute-start.3 = (bf16[520,1024]{1,0:T(8,128)(2,1)}, bf16[520,1024]{1,0:T(8,128)(2,1)S(1)}, u32[]{:S(2)}, u32[]{:S(2)}) collective-permute-start(bf16[520,1024]{1,0:T(8,128)(2,1)} %get-tuple-element.69), channel_id=1, source_target_pairs={{0,8},{8,0},{16,24},{24,16},{1,9},{9,1},{17,25},{25,17},{2,10},{10... | collective-permute-start | bytes 3194888 | tf_op jit(solution)/shard_map/ppermute | solution.py:481
  50.6 8.3 %copy-start.3 = (f32[512,1024]{1,0:T(8,128)S(1)}, f32[512,1024]{1,0:T(8,128)}, u32[]{:S(2)}) copy-start(f32[512,1024]{1,0:T(8,128)} %get-tuple-element.73) | copy-start | bytes 6291460
  59.0 0.7 copy-start.5
  59.9 15.6 %collective-permute-start.4 = (bf16[136,1024]{1,0:T(8,128)(2,1)S(1)}, bf16[136,1024]{1,0:T(8,128)(2,1)S(1)}, u32[]{:S(2)}, u32[]{:S(2)}) collective-permute-start(bf16[136,1024]{1,0:T(8,128)(2,1)S(1)} %get-tuple-element.78), channel_id=1, source_target_pairs={{0,64},{8,24},{16,80},{24,40},{32,96},{40,56},{48,112},{56,8},{64,... | collective-permute-start | bytes 835592 | tf_op jit(solution)/shard_map/ppermute | solution.py:486
  60.2 15.3 %collective-permute-start.5 = (bf16[136,1024]{1,0:T(8,128)(2,1)S(1)}, bf16[136,1024]{1,0:T(8,128)(2,1)S(1)}, u32[]{:S(2)}, u32[]{:S(2)}) collective-permute-start(bf16[136,1024]{1,0:T(8,128)(2,1)S(1)} %get-tuple-element.79), channel_id=1, source_target_pairs={{0,128},{8,40},{16,144},{24,56},{32,160},{40,8},{48,176},{56,24},{... | collective-permute-start | bytes 835592 | tf_op jit(solution)/shard_map/ppermute | solution.py:486
  63.0 12.5 %collective-permute-start.6 = (bf16[136,1024]{1,0:T(8,128)(2,1)S(1)}, bf16[136,1024]{1,0:T(8,128)(2,1)S(1)}, u32[]{:S(2)}, u32[]{:S(2)}) collective-permute-start(bf16[136,1024]{1,0:T(8,128)(2,1)S(1)} %get-tuple-element.80), channel_id=1, source_target_pairs={{0,192},{8,56},{16,208},{24,8},{32,224},{40,24},{48,240},{56,40},{... | collective-permute-start | bytes 835592 | tf_op jit(solution)/shard_map/ppermute | solution.py:486
  75.8 22.3 %collective-permute-start.10 = (bf16[512,3072]{1,0:T(8,128)(2,1)}, bf16[512,3072]{1,0:T(8,128)(2,1)}, u32[]{:S(2)}, u32[]{:S(2)}) collective-permute-start(bf16[512,3072]{1,0:T(8,128)(2,1)} %all-gather.2.cloned.1.call-done.refs_9_), channel_id=1, source_target_pairs={{0,8},{8,0},{16,24},{24,16},{1,9},{9,1},{17,25},{25,17},{2,10},{10... | collective-permute-start | bytes 9437192 | tf_op jit(solution)/shard_map/ppermute | solution.py:479
  76.1 14.7 %collective-permute-start.7 = (bf16[40,1024]{1,0:T(8,128)(2,1)S(1)}, bf16[40,1024]{1,0:T(8,128)(2,1)S(1)}, u32[]{:S(2)}, u32[]{:S(2)}) collective-permute-start(bf16[40,1024]{1,0:T(8,128)(2,1)S(1)} %get-tuple-element.89), channel_id=1, source_target_pairs={{0,16},{8,72},{16,32},{24,88},{32,48},{40,104},{48,0},{56,120},{64... | collective-permute-start | bytes 245768 | tf_op jit(solution)/shard_map/ppermute | solution.py:486
  76.2 14.6 %collective-permute-start.8 = (bf16[40,1024]{1,0:T(8,128)(2,1)S(1)}, bf16[40,1024]{1,0:T(8,128)(2,1)S(1)}, u32[]{:S(2)}, u32[]{:S(2)}) collective-permute-start(bf16[40,1024]{1,0:T(8,128)(2,1)S(1)} %get-tuple-element.90), channel_id=1, source_target_pairs={{0,32},{8,136},{16,48},{24,152},{32,0},{40,168},{48,16},{56,184},{... | collective-permute-start | bytes 245768 | tf_op jit(solution)/shard_map/ppermute | solution.py:486
  77.9 12.9 %collective-permute-start.9 = (bf16[40,1024]{1,0:T(8,128)(2,1)S(1)}, bf16[40,1024]{1,0:T(8,128)(2,1)S(1)}, u32[]{:S(2)}, u32[]{:S(2)}) collective-permute-start(bf16[40,1024]{1,0:T(8,128)(2,1)S(1)} %get-tuple-element.91), channel_id=1, source_target_pairs={{0,48},{8,200},{16,0},{24,216},{32,16},{40,232},{48,32},{56,248},{... | collective-permute-start | bytes 245768 | tf_op jit(solution)/shard_map/ppermute | solution.py:486
  91.1 15.0 %collective-permute-start.11 = (bf16[24,1024]{1,0:T(8,128)(2,1)S(1)}, bf16[24,1024]{1,0:T(8,128)(2,1)S(1)}, u32[]{:S(2)}, u32[]{:S(2)}) collective-permute-start(bf16[24,1024]{1,0:T(8,128)(2,1)S(1)} %pad_maximum_fusion.6), channel_id=1, source_target_pairs={{0,4},{1,5},{2,6},{3,7},{4,0},{5,1},{6,2},{7,3},{8,12},{9,13},{10,... | collective-permute-start | bytes 147464 | tf_op jit(solution)/shard_map/ppermute | solution.py:499
  106.3 5.8 %collective-permute-start.14 = (bf16[16,1024]{1,0:T(8,128)(2,1)S(1)}, bf16[16,1024]{1,0:T(8,128)(2,1)S(1)}, u32[]{:S(2)}, u32[]{:S(2)}) collective-permute-start(bf16[16,1024]{1,0:T(8,128)(2,1)S(1)} %pad_maximum_fusion.7), channel_id=1, source_target_pairs={{0,2},{1,3},{2,0},{3,1},{4,6},{5,7},{6,4},{7,5},{8,10},{9,11},{10,... | collective-permute-start | bytes 98312 | tf_op jit(solution)/shard_map/ppermute | solution.py:499
  107.6 6.5 %collective-permute-start.15 = (bf16[144,1024]{1,0:T(8,128)(2,1)}, bf16[144,1024]{1,0:T(8,128)(2,1)S(1)}, u32[]{:S(2)}, u32[]{:S(2)}) collective-permute-start(bf16[144,1024]{1,0:T(8,128)(2,1)} %get-tuple-element.113), channel_id=1, source_target_pairs={{0,8},{8,16},{16,24},{24,0},{1,9},{9,17},{17,25},{25,1},{2,10},{10... | collective-permute-start | bytes 884744 | tf_op jit(solution)/shard_map/ppermute | solution.py:430
  108.9 14.3 %collective-permute-start.12 = (bf16[144,1024]{1,0:T(8,128)(2,1)}, bf16[144,1024]{1,0:T(8,128)(2,1)S(1)}, u32[]{:S(2)}, u32[]{:S(2)}) collective-permute-start(bf16[144,1024]{1,0:T(8,128)(2,1)} %get-tuple-element.110), channel_id=1, source_target_pairs={{0,40},{8,48},{16,56},{24,32},{32,72},{40,80},{48,88},{56,64},{64,... | collective-permute-start | bytes 884744 | tf_op jit(solution)/shard_map/ppermute | solution.py:428
  109.9 16.1 %collective-permute-start.13 = (bf16[144,1024]{1,0:T(8,128)(2,1)}, bf16[144,1024]{1,0:T(8,128)(2,1)S(1)}, u32[]{:S(2)}, u32[]{:S(2)}) collective-permute-start(bf16[144,1024]{1,0:T(8,128)(2,1)} %get-tuple-element.111), channel_id=1, source_target_pairs={{0,32},{32,64},{64,96},{96,128},{128,160},{160,192},{192,224},{224... | collective-permute-start | bytes 884744 | tf_op jit(solution)/shard_map/ppermute | solution.py:430
  114.1 13.8 %collective-permute-start.16 = (bf16[12,1024]{1,0:T(8,128)(2,1)S(1)}, bf16[12,1024]{1,0:T(8,128)(2,1)S(1)}, u32[]{:S(2)}, u32[]{:S(2)}) collective-permute-start(bf16[12,1024]{1,0:T(8,128)(2,1)S(1)} %pad_maximum_fusion.8), channel_id=1, source_target_pairs={{0,1},{1,0},{2,3},{3,2},{4,5},{5,4},{6,7},{7,6},{8,9},{9,8},{10,11... | collective-permute-start | bytes 73736 | tf_op jit(solution)/shard_map/ppermute | solution.py:499
  115.1 11.4 %copy-start.2 = (bf16[1,24,24,1024]{3,2,1,0:T(8,128)(2,1)S(1)}, bf16[1,24,24,1024]{3,2,1,0:T(8,128)(2,1)}, u32[]{:S(2)}) copy-start(bf16[1,24,24,1024]{3,2,1,0:T(8,128)(2,1)} %param.7) | copy-start | bytes 3538948
  126.3 2.9 %copy-start.1 = (bf16[128,3072]{1,0:T(8,128)(2,1)S(1)}, bf16[128,3072]{1,0:T(8,128)(2,1)}, u32[]{:S(2)}) copy-start(bf16[128,3072]{1,0:T(8,128)(2,1)} %param.8) | copy-start | bytes 2359300
Sparse Core Ops, SparseCore 0:
  18.2 44.7 all-gather.1

commit v2 on v1

--- a/solution.py
+++ b/solution.py
@@ -329,12 +329,12 @@
         ).astype(BF)
 
 
-def back_product(parts, mine, other, core):
+def back_product(parts, mine, other, core, which):
     tokens = parts[0].shape[0]
     rows, inner = mine.shape
-    steps = 4
-    wide = 2 * rows // steps
-    side = pl.BlockSpec((rows // steps, inner), lambda g: (g, 0))
+    steps = 2
+    wide = 2 * rows // (2 * steps)
+    side = pl.BlockSpec((rows // (2 * steps), inner), lambda g: (g + which * steps, 0))
     out = pl.BlockSpec((tokens // 4, wide), lambda g: (0, g))
     return pl.pallas_call(
         back_kernel,
@@ -346,7 +346,7 @@
         out_shape=[shape(tokens // 4, wide * steps)(BF)] * 4,
         compiler_params=params(),
         cost_estimate=pl.CostEstimate(
-            flops=6_000_000_000, bytes_accessed=12_000_000, transcendentals=0
+            flops=3_000_000_000, bytes_accessed=8_000_000, transcendentals=0
         ),
         name="back_product",
     )(core, *parts, mine, other)
@@ -524,21 +524,29 @@
     got = swap(piece, 4)
 
     parts = [part for trio in zip(part_a, part_b, part_c) for part in trio]
-    quarters = back_product(parts, mine, other, bit)
+    def halos(quarters):
+        return [quarters[0]] + [
+            shift(quarters[i], i // 2 == 1, i % 2 == 1, 1) for i in (1, 2, 3)
+        ]
+
+    quarters = back_product(parts, mine, other, bit, 0)
     quarters, got = lax.optimization_barrier((quarters, got))
-    local, to_col, to_row, to_both = [quarters[0]] + [
-        shift(quarters[i], i // 2 == 1, i % 2 == 1, 1) for i in (1, 2, 3)
-    ]
+    moved = [halos(quarters)]
     sums, gain = round_sums([got], own, gain, index)
     piece, own, gain, index = halve(sums, gain, 2)
-    sums, gain = round_sums([swap(piece, 2)], own, gain, index)
-    sums, to_col = lax.optimization_barrier((sums, to_col))
+    parts, piece = lax.optimization_barrier((parts, piece))
+    got = swap(piece, 2)
+    quarters = back_product(parts, mine, other, bit, 1)
+    quarters, got, moved[0][2:] = lax.optimization_barrier((quarters, got, moved[0][2:]))
+    moved.append(halos(quarters))
+    sums, gain = round_sums([got], own, gain, index)
     piece, own, gain, index = halve(sums, gain, 1)
     sums, gain = round_sums([swap(piece, 1)], own, gain, index)
     grad_proj, grad_gain = sums * norm, gain * norm
+    grad_proj, grad_gain, moved[1] = lax.optimization_barrier((grad_proj, grad_gain, moved[1]))
 
     local, to_col, to_row, to_both = (
-        part.reshape(square) for part in (local, to_col, to_row, to_both)
+        jnp.concatenate(pair, axis=1).reshape(square) for pair in zip(*moved)
     )
     moved = jnp.concatenate(
         [

time: 136 us -> 143 us (1.051)
  starting transfers between devices: 29.4 us -> 33 us
  Pallas kernels: 68 us -> 70.8 us
    pallas_call x1 -> x2, Pallas kernels: 8.03 us -> 10.9 us  [back_product(): pl.pallas_call(back_kernel, grid=(steps,), in_specs=[pl.BlockSpec(memory_...]
    ppermute x2 -> x3, starting transfers between devices: 2.29 us -> 5.12 us  [shift(): return lax.ppermute(value, ('row', 'col'), pairs)]
    ppermute x4 -> x6, starting transfers between devices: 9.23 us -> 10.1 us  [shift(): lax.ppermute(value, name, [(i, (i + step) % count) for i in range(count)])]
    ppermute x2 -> x3, waiting for transfers between devices: 8.07 us -> 8.21 us  [shift(): return lax.ppermute(value, ('row', 'col'), pairs)]
    ppermute x4 -> x6, waiting for transfers between devices: 4.68 us -> 4.73 us  [shift(): lax.ppermute(value, name, [(i, (i + step) % count) for i in range(count)])]
  transfers between devices with their start and end apart: 18 -> 21, of which waited for: 3 -> 4; matrix products, arithmetic and copies ran while one was open for 6% -> 4% of each run, Pallas kernels for 50% -> 50%
where the time goes in v2:
time: 143 us
  Pallas kernels  70.8 us (50%)
  starting transfers between devices  33 us (23%)
  between operations  14.6 us (10%)
  waiting for transfers between devices  13 us (9%)
  other arithmetic  6.47 us (5%)
  local copies, waits for them, and re-layouts  4.73 us (3%)
    pallas_call x3, Pallas kernels, backward(): pl.pallas_call(backward_kernel, grid=(count,), in_specs=[pl.BlockSpec((GR...  30 us
    pallas_call x1, Pallas kernels, forward(): pl.pallas_call(forward_kernel, grid=(per,), in_specs=[column_block(tokens...  20.2 us
    pallas_call x2, Pallas kernels, back_product(): pl.pallas_call(back_kernel, grid=(steps,), in_specs=[pl.BlockSpec(memory_...  10.9 us
    ppermute x6, starting transfers between devices, shift(): lax.ppermute(value, name, [(i, (i + step) % count) for i in range(count)])  10.1 us
    pallas_call x1, Pallas kernels, middle(): pl.pallas_call(lambda *refs: middle_kernel(order, *refs), in_specs=[pl.Bl...  9.69 us
    ppermute x3, starting transfers between devices, swap(): return lax.ppermute(piece, 'dp', [(i, i ^ bit) for i in range(d)])  9.08 us
    ppermute x6, starting transfers between devices, plane_round(): lax.ppermute(piece, ('row', 'col'), plane_pairs(r, c, turn, n + 1))  8.56 us
    ppermute x3, waiting for transfers between devices, shift(): return lax.ppermute(value, ('row', 'col'), pairs)  8.21 us
  transfers between devices with their start and end apart: 21, of which 4 were waited for; matrix products, arithmetic and copies ran while one was open for 4% of the time, Pallas kernels for 50%

profile of v2, /device:TPU:1, one launch (start us, length us, event | category | flops | bytes accessed | tf_op | source)
XLA Modules:
  0.0 142.6 jit_solution(3511167705143105667)
XLA Ops:
  7.2 1.7 %fusion.15 = (bf16[12,12,1024]{2,1,0:T(8,128)(2,1)S(1)}, bf16[12,12,1024]{2,1,0:T(8,128)(2,1)S(1)}, bf16[12,12,1024]{2,1,0:T(8,128)(2,1)S(1)}, bf16[12,12,1024]{2,1,0:T(8,128)(2,1)S(1)}) fusion(bf16[24,24,1024]{2,1,0:T(8,128)(2,1)} %bitcast.32), kind=kLoop, calls=%fused_computation.83 | loop fusion | bytes 2359296 | tf_op jit(solution)/shard_map/slice | solution.py:437
  9.0 3.3 %collective-permute-start = (bf16[144,1024]{1,0:T(8,128)(2,1)S(1)}, bf16[144,1024]{1,0:T(8,128)(2,1)S(1)}, u32[]{:S(2)}, u32[]{:S(2)}) collective-permute-start(bf16[144,1024]{1,0:T(8,128)(2,1)S(1)} %reshape.78), channel_id=1, source_target_pairs={{0,24},{8,0},{16,8},{24,16},{1,25},{9,1},{17,9},{25,17},{2,26},{10... | collective-permute-start | bytes 884744 | tf_op jit(solution)/shard_map/ppermute | solution.py:430
  12.4 3.5 %collective-permute-start.1 = (bf16[144,1024]{1,0:T(8,128)(2,1)S(1)}, bf16[144,1024]{1,0:T(8,128)(2,1)S(1)}, u32[]{:S(2)}, u32[]{:S(2)}) collective-permute-start(bf16[144,1024]{1,0:T(8,128)(2,1)S(1)} %reshape.80), channel_id=1, source_target_pairs={{0,224},{32,0},{64,32},{96,64},{128,96},{160,128},{192,160},{224,1... | collective-permute-start | bytes 884744 | tf_op jit(solution)/shard_map/ppermute | solution.py:430
  16.0 1.3 collective-permute-start.2
  19.0 20.2 %attn_forward.1 = (bf16[32,576,512]{2,1,0:T(8,128)(2,1)}, bf16[576,2048]{1,0:T(8,128)(2,1)}, f32[576,1024]{1,0:T(8,128)}, f32[576,1024]{1,0:T(8,128)}) custom-call(bf16[576,3072]{1,0:T(8,128)(2,1)} %bitcast.20, bf16[576,3072]{1,0:T(8,128)(2,1)} %bitcast.21, bf16[576,3072]{1,0:T(8,128)(2,1)} %bitcast.22, bf16[576,128]{1,0:T(8,128)(2,1)} %fusion.hot_ref), custom_call_target="tpu_custom_call" | custom-call | flops 25600000000 | bytes 32000000 | tf_op jit(solution)/shard_map/attn_forward/pallas_call | solution.py:208
  39.5 1.4 maximum_maximum_fusion
  40.9 9.7 %middle.1 = (bf16[576,1024]{1,0:T(8,128)(2,1)}, bf16[520,1024]{1,0:T(8,128)(2,1)}, f32[512,1024]{1,0:T(8,128)}, f32[1,1024]{1,0:T(1,128)}) custom-call(s32[1]{0:T(128)} %bitcast.refs_0_.core_ref, f32[576,1024]{1,0:T(8,128)} %get-tuple-element.88.refs_1_.o_ref, bf16[1024,1024]{1,0:T(8,128)(2,1)} %refs_2_.1, bf16[576,1024]{1,0:T(8,128)(2,1)} %bitcast.33, ...), custom_call_target="tpu_custom_call" | custom-call | flops 8000000000 | bytes 16000000 | tf_op jit(solution)/shard_map/middle/pallas_call | solution.py:294
  50.6 8.3 %attn_backward.3 = (bf16[576,256]{1,0:T(8,128)(2,1)}, bf16[576,256]{1,0:T(8,128)(2,1)}, bf16[576,256]{1,0:T(8,128)(2,1)}) custom-call(bf16[32,576,512]{2,1,0:T(8,128)(2,1)} %get-tuple-element.86.p_ref, bf16[576,2048]{1,0:T(8,128)(2,1)} %get-tuple-element.87.rest_ref, bf16[576,3072]{1,0:T(8,128)(2,1)} %bitcast.23, bf16[576,3072]{1,0:T(8,128)(2,1)} %bitcast.24, ...), custom_call_target="tpu_custom_call" | custom-call | flops 7200000000 | bytes 8000000 | tf_op jit(solution)/shard_map/attn_backward/pallas_call | solution.py:235
  60.2 2.8 %collective-permute-start.5 = (bf16[136,1024]{1,0:T(8,128)(2,1)S(1)}, bf16[136,1024]{1,0:T(8,128)(2,1)S(1)}, u32[]{:S(2)}, u32[]{:S(2)}) collective-permute-start(bf16[136,1024]{1,0:T(8,128)(2,1)S(1)} %get-tuple-element.104), channel_id=1, source_target_pairs={{0,128},{8,40},{16,144},{24,56},{32,160},{40,8},{48,176},{56,24},{... | collective-permute-start | bytes 835592 | tf_op jit(solution)/shard_map/ppermute | solution.py:486
  62.9 1.6 %collective-permute-start.6 = (bf16[136,1024]{1,0:T(8,128)(2,1)S(1)}, bf16[136,1024]{1,0:T(8,128)(2,1)S(1)}, u32[]{:S(2)}, u32[]{:S(2)}) collective-permute-start(bf16[136,1024]{1,0:T(8,128)(2,1)S(1)} %get-tuple-element.105), channel_id=1, source_target_pairs={{0,192},{8,56},{16,208},{24,8},{32,224},{40,24},{48,240},{56,40},{... | collective-permute-start | bytes 835592 | tf_op jit(solution)/shard_map/ppermute | solution.py:486
  64.6 10.8 %attn_backward.4 = (bf16[576,384]{1,0:T(8,128)(2,1)}, bf16[576,384]{1,0:T(8,128)(2,1)}, bf16[576,384]{1,0:T(8,128)(2,1)}) custom-call(bf16[32,576,512]{2,1,0:T(8,128)(2,1)} %get-tuple-element.86.p_ref, bf16[576,2048]{1,0:T(8,128)(2,1)} %get-tuple-element.87.rest_ref, bf16[576,3072]{1,0:T(8,128)(2,1)} %bitcast.26, bf16[576,3072]{1,0:T(8,128)(2,1)} %bitcast.27, ...), custom_call_target="tpu_custom_call" | custom-call | flops 10800000000 | bytes 12000000 | tf_op jit(solution)/shard_map/attn_backward/pallas_call | solution.py:235
  76.1 1.7 %collective-permute-start.8 = (bf16[40,1024]{1,0:T(8,128)(2,1)S(1)}, bf16[40,1024]{1,0:T(8,128)(2,1)S(1)}, u32[]{:S(2)}, u32[]{:S(2)}) collective-permute-start(bf16[40,1024]{1,0:T(8,128)(2,1)S(1)} %get-tuple-element.115), channel_id=1, source_target_pairs={{0,32},{8,136},{16,48},{24,152},{32,0},{40,168},{48,16},{56,184},{... | collective-permute-start | bytes 245768 | tf_op jit(solution)/shard_map/ppermute | solution.py:486
  77.9 2.0 %collective-permute-start.9 = (bf16[40,1024]{1,0:T(8,128)(2,1)S(1)}, bf16[40,1024]{1,0:T(8,128)(2,1)S(1)}, u32[]{:S(2)}, u32[]{:S(2)}) collective-permute-start(bf16[40,1024]{1,0:T(8,128)(2,1)S(1)} %get-tuple-element.116), channel_id=1, source_target_pairs={{0,48},{8,200},{16,0},{24,216},{32,16},{40,232},{48,32},{56,248},{... | collective-permute-start | bytes 245768 | tf_op jit(solution)/shard_map/ppermute | solution.py:486
  79.8 10.9 %attn_backward.5 = (bf16[576,384]{1,0:T(8,128)(2,1)}, bf16[576,384]{1,0:T(8,128)(2,1)}, bf16[576,384]{1,0:T(8,128)(2,1)}) custom-call(bf16[32,576,512]{2,1,0:T(8,128)(2,1)} %get-tuple-element.86.p_ref, bf16[576,2048]{1,0:T(8,128)(2,1)} %get-tuple-element.87.rest_ref, bf16[576,3072]{1,0:T(8,128)(2,1)} %bitcast.29, bf16[576,3072]{1,0:T(8,128)(2,1)} %bitcast.30, ...), custom_call_target="tpu_custom_call" | custom-call | flops 10800000000 | bytes 12000000 | tf_op jit(solution)/shard_map/attn_backward/pallas_call | solution.py:235
  91.0 7.0 %collective-permute-start.11 = (bf16[24,1024]{1,0:T(8,128)(2,1)S(1)}, bf16[24,1024]{1,0:T(8,128)(2,1)S(1)}, u32[]{:S(2)}, u32[]{:S(2)}) collective-permute-start(bf16[24,1024]{1,0:T(8,128)(2,1)S(1)} %pad_maximum_fusion.10), channel_id=1, source_target_pairs={{0,4},{1,5},{2,6},{3,7},{4,0},{5,1},{6,2},{7,3},{8,12},{9,13},{10,... | collective-permute-start | bytes 147464 | tf_op jit(solution)/shard_map/ppermute | solution.py:499
  98.0 5.4 %back_product.2 = (bf16[144,512]{1,0:T(8,128)(2,1)}, bf16[144,512]{1,0:T(8,128)(2,1)}, bf16[144,512]{1,0:T(8,128)(2,1)}, bf16[144,512]{1,0:T(8,128)(2,1)}) custom-call(s32[1]{0:T(128)} %bitcast.refs_0_.core_ref, bf16[576,256]{1,0:T(8,128)(2,1)} %get-tuple-element.136.refs_0_, bf16[576,384]{1,0:T(8,128)(2,1)} %get-tuple-element.137.refs_1_, ...), custom_call_target="tpu_custom_call" | custom-call | flops 3000000000 | bytes 8000000 | tf_op jit(solution)/shard_map/back_product/pallas_call | solution.py:339
  104.9 2.6 %collective-permute-start.13 = (bf16[144,512]{1,0:T(8,128)(2,1)}, bf16[144,512]{1,0:T(8,128)(2,1)S(1)}, u32[]{:S(2)}, u32[]{:S(2)}) collective-permute-start(bf16[144,512]{1,0:T(8,128)(2,1)} %get-tuple-element.150), channel_id=1, source_target_pairs={{0,32},{32,64},{64,96},{96,128},{128,160},{160,192},{192,224},{224... | collective-permute-start | bytes 442376 | tf_op jit(solution)/shard_map/ppermute | solution.py:430
  107.6 1.7 %collective-permute-start.14 = (bf16[144,512]{1,0:T(8,128)(2,1)}, bf16[144,512]{1,0:T(8,128)(2,1)S(1)}, u32[]{:S(2)}, u32[]{:S(2)}) collective-permute-start(bf16[144,512]{1,0:T(8,128)(2,1)} %get-tuple-element.151), channel_id=1, source_target_pairs={{0,40},{8,48},{16,56},{24,32},{32,72},{40,80},{48,88},{56,64},{64,... | collective-permute-start | bytes 442376 | tf_op jit(solution)/shard_map/ppermute | solution.py:428
  109.2 5.4 %back_product.3 = (bf16[144,512]{1,0:T(8,128)(2,1)}, bf16[144,512]{1,0:T(8,128)(2,1)}, bf16[144,512]{1,0:T(8,128)(2,1)}, bf16[144,512]{1,0:T(8,128)(2,1)}) custom-call(s32[1]{0:T(128)} %bitcast.refs_0_.core_ref, bf16[576,256]{1,0:T(8,128)(2,1)} %get-tuple-element.136.refs_0_, bf16[576,384]{1,0:T(8,128)(2,1)} %get-tuple-element.137.refs_1_, ...), custom_call_target="tpu_custom_call" | custom-call | flops 3000000000 | bytes 8000000 | tf_op jit(solution)/shard_map/back_product/pallas_call | solution.py:339
  114.7 3.8 %collective-permute-done.14 = bf16[144,512]{1,0:T(8,128)(2,1)S(1)} collective-permute-done((bf16[144,512]{1,0:T(8,128)(2,1)}, bf16[144,512]{1,0:T(8,128)(2,1)S(1)}, u32[]{:S(2)}, u32[]{:S(2)}) %collective-permute-start.14) | collective-permute-done | bytes 147488 | tf_op jit(solution)/shard_map/ppermute | solution.py:428
  120.2 2.1 %collective-permute-start.18 = (bf16[144,512]{1,0:T(8,128)(2,1)}, bf16[144,512]{1,0:T(8,128)(2,1)S(1)}, u32[]{:S(2)}, u32[]{:S(2)}) collective-permute-start(bf16[144,512]{1,0:T(8,128)(2,1)} %get-tuple-element.157), channel_id=1, source_target_pairs={{0,40},{8,48},{16,56},{24,32},{32,72},{40,80},{48,88},{56,64},{64,... | collective-permute-start | bytes 442376 | tf_op jit(solution)/shard_map/ppermute | solution.py:428
  124.6 3.7 %collective-permute-done.17 = bf16[144,512]{1,0:T(8,128)(2,1)S(1)} collective-permute-done((bf16[144,512]{1,0:T(8,128)(2,1)}, bf16[144,512]{1,0:T(8,128)(2,1)S(1)}, u32[]{:S(2)}, u32[]{:S(2)}) %collective-permute-start.17) | collective-permute-done | bytes 147488 | tf_op jit(solution)/shard_map/ppermute | solution.py:430
  128.3 4.4 %collective-permute-done.18 = bf16[144,512]{1,0:T(8,128)(2,1)S(1)} collective-permute-done((bf16[144,512]{1,0:T(8,128)(2,1)}, bf16[144,512]{1,0:T(8,128)(2,1)S(1)}, u32[]{:S(2)}, u32[]{:S(2)}) %collective-permute-start.18) | collective-permute-done | bytes 147488 | tf_op jit(solution)/shard_map/ppermute | solution.py:428
  134.3 1.5 %add_convert_fusion = bf16[1,24,24,1024]{3,2,1,0:T(8,128)(2,1)} fusion(bf16[1,24,24,1024]{3,2,1,0:T(8,128)(2,1)S(1)} %copy-done.2, bf16[1,12,24,1024]{3,2,1,0:T(8,128)(2,1)S(1)} %maximum_bitcast_fusion.1, bf16[1,12,24,1024]{3,2,1,0:T(8,128)(2,1)S(1)} %maximum_bitcast_fusion), kind=kLoop, calls=%fused_computation | loop fusion | flops 2949120 | bytes 3538944 | tf_op jit(solution)/shard_map/convert_element_type | solution.py:558
  (109 shorter events, 11.1 us)
Async XLA Ops:
  7.2 68.6 %all-gather.2.cloned.1.call-start = ((), (), s32[]{:S(2)}) async-start(), calls=%async_computation | async-start | bytes 3538944 | tf_op jit(solution)/shard_map/all_gather | solution.py:454
  9.0 30.2 %collective-permute-start = (bf16[144,1024]{1,0:T(8,128)(2,1)S(1)}, bf16[144,1024]{1,0:T(8,128)(2,1)S(1)}, u32[]{:S(2)}, u32[]{:S(2)}) collective-permute-start(bf16[144,1024]{1,0:T(8,128)(2,1)S(1)} %reshape.78), channel_id=1, source_target_pairs={{0,24},{8,0},{16,8},{24,16},{1,25},{9,1},{17,9},{25,17},{2,26},{10... | collective-permute-start | bytes 884744 | tf_op jit(solution)/shard_map/ppermute | solution.py:430
  12.4 26.9 %collective-permute-start.1 = (bf16[144,1024]{1,0:T(8,128)(2,1)S(1)}, bf16[144,1024]{1,0:T(8,128)(2,1)S(1)}, u32[]{:S(2)}, u32[]{:S(2)}) collective-permute-start(bf16[144,1024]{1,0:T(8,128)(2,1)S(1)} %reshape.80), channel_id=1, source_target_pairs={{0,224},{32,0},{64,32},{96,64},{128,96},{160,128},{192,160},{224,1... | collective-permute-start | bytes 884744 | tf_op jit(solution)/shard_map/ppermute | solution.py:430
  16.0 23.5 %collective-permute-start.2 = (bf16[144,1024]{1,0:T(8,128)(2,1)S(1)}, bf16[144,1024]{1,0:T(8,128)(2,1)S(1)}, u32[]{:S(2)}, u32[]{:S(2)}) collective-permute-start(bf16[144,1024]{1,0:T(8,128)(2,1)S(1)} %reshape.82), channel_id=1, source_target_pairs={{0,248},{8,224},{16,232},{24,240},{32,24},{40,0},{48,8},{56,16},{6... | collective-permute-start | bytes 884744 | tf_op jit(solution)/shard_map/ppermute | solution.py:428
  50.6 8.4 %collective-permute-start.3 = (bf16[520,1024]{1,0:T(8,128)(2,1)}, bf16[520,1024]{1,0:T(8,128)(2,1)S(1)}, u32[]{:S(2)}, u32[]{:S(2)}) collective-permute-start(bf16[520,1024]{1,0:T(8,128)(2,1)} %get-tuple-element.94), channel_id=1, source_target_pairs={{0,8},{8,0},{16,24},{24,16},{1,9},{9,1},{17,25},{25,17},{2,10},{10... | collective-permute-start | bytes 3194888 | tf_op jit(solution)/shard_map/ppermute | solution.py:481
  59.8 15.6 %collective-permute-start.4 = (bf16[136,1024]{1,0:T(8,128)(2,1)S(1)}, bf16[136,1024]{1,0:T(8,128)(2,1)S(1)}, u32[]{:S(2)}, u32[]{:S(2)}) collective-permute-start(bf16[136,1024]{1,0:T(8,128)(2,1)S(1)} %get-tuple-element.103), channel_id=1, source_target_pairs={{0,64},{8,24},{16,80},{24,40},{32,96},{40,56},{48,112},{56,8},{64,... | collective-permute-start | bytes 835592 | tf_op jit(solution)/shard_map/ppermute | solution.py:486
  60.2 15.2 %collective-permute-start.5 = (bf16[136,1024]{1,0:T(8,128)(2,1)S(1)}, bf16[136,1024]{1,0:T(8,128)(2,1)S(1)}, u32[]{:S(2)}, u32[]{:S(2)}) collective-permute-start(bf16[136,1024]{1,0:T(8,128)(2,1)S(1)} %get-tuple-element.104), channel_id=1, source_target_pairs={{0,128},{8,40},{16,144},{24,56},{32,160},{40,8},{48,176},{56,24},{... | collective-permute-start | bytes 835592 | tf_op jit(solution)/shard_map/ppermute | solution.py:486
  62.9 12.5 %collective-permute-start.6 = (bf16[136,1024]{1,0:T(8,128)(2,1)S(1)}, bf16[136,1024]{1,0:T(8,128)(2,1)S(1)}, u32[]{:S(2)}, u32[]{:S(2)}) collective-permute-start(bf16[136,1024]{1,0:T(8,128)(2,1)S(1)} %get-tuple-element.105), channel_id=1, source_target_pairs={{0,192},{8,56},{16,208},{24,8},{32,224},{40,24},{48,240},{56,40},{... | collective-permute-start | bytes 835592 | tf_op jit(solution)/shard_map/ppermute | solution.py:486
  75.8 22.3 %collective-permute-start.10 = (bf16[512,3072]{1,0:T(8,128)(2,1)}, bf16[512,3072]{1,0:T(8,128)(2,1)}, u32[]{:S(2)}, u32[]{:S(2)}) collective-permute-start(bf16[512,3072]{1,0:T(8,128)(2,1)} %all-gather.2.cloned.1.call-done.refs_9_), channel_id=1, source_target_pairs={{0,8},{8,0},{16,24},{24,16},{1,9},{9,1},{17,25},{25,17},{2,10},{10... | collective-permute-start | bytes 9437192 | tf_op jit(solution)/shard_map/ppermute | solution.py:479
  76.0 14.7 %collective-permute-start.7 = (bf16[40,1024]{1,0:T(8,128)(2,1)S(1)}, bf16[40,1024]{1,0:T(8,128)(2,1)S(1)}, u32[]{:S(2)}, u32[]{:S(2)}) collective-permute-start(bf16[40,1024]{1,0:T(8,128)(2,1)S(1)} %get-tuple-element.114), channel_id=1, source_target_pairs={{0,16},{8,72},{16,32},{24,88},{32,48},{40,104},{48,0},{56,120},{64... | collective-permute-start | bytes 245768 | tf_op jit(solution)/shard_map/ppermute | solution.py:486
  76.1 14.6 %collective-permute-start.8 = (bf16[40,1024]{1,0:T(8,128)(2,1)S(1)}, bf16[40,1024]{1,0:T(8,128)(2,1)S(1)}, u32[]{:S(2)}, u32[]{:S(2)}) collective-permute-start(bf16[40,1024]{1,0:T(8,128)(2,1)S(1)} %get-tuple-element.115), channel_id=1, source_target_pairs={{0,32},{8,136},{16,48},{24,152},{32,0},{40,168},{48,16},{56,184},{... | collective-permute-start | bytes 245768 | tf_op jit(solution)/shard_map/ppermute | solution.py:486
  77.9 12.9 %collective-permute-start.9 = (bf16[40,1024]{1,0:T(8,128)(2,1)S(1)}, bf16[40,1024]{1,0:T(8,128)(2,1)S(1)}, u32[]{:S(2)}, u32[]{:S(2)}) collective-permute-start(bf16[40,1024]{1,0:T(8,128)(2,1)S(1)} %get-tuple-element.116), channel_id=1, source_target_pairs={{0,48},{8,200},{16,0},{24,216},{32,16},{40,232},{48,32},{56,248},{... | collective-permute-start | bytes 245768 | tf_op jit(solution)/shard_map/ppermute | solution.py:486
  91.0 12.4 %collective-permute-start.11 = (bf16[24,1024]{1,0:T(8,128)(2,1)S(1)}, bf16[24,1024]{1,0:T(8,128)(2,1)S(1)}, u32[]{:S(2)}, u32[]{:S(2)}) collective-permute-start(bf16[24,1024]{1,0:T(8,128)(2,1)S(1)} %pad_maximum_fusion.10), channel_id=1, source_target_pairs={{0,4},{1,5},{2,6},{3,7},{4,0},{5,1},{6,2},{7,3},{8,12},{9,13},{10,... | collective-permute-start | bytes 147464 | tf_op jit(solution)/shard_map/ppermute | solution.py:499
  103.6 15.9 %copy-start.8 = (bf16[144,512]{1,0:T(8,128)(2,1)S(1)}, bf16[144,512]{1,0:T(8,128)(2,1)}, u32[]{:S(2)}) copy-start(bf16[144,512]{1,0:T(8,128)(2,1)} %get-tuple-element.161) | copy-start | bytes 442372
  103.6 11.1 %collective-permute-start.12 = (bf16[16,1024]{1,0:T(8,128)(2,1)S(1)}, bf16[16,1024]{1,0:T(8,128)(2,1)S(1)}, u32[]{:S(2)}, u32[]{:S(2)}) collective-permute-start(bf16[16,1024]{1,0:T(8,128)(2,1)S(1)} %pad_maximum_fusion.11), channel_id=1, source_target_pairs={{0,2},{1,3},{2,0},{3,1},{4,6},{5,7},{6,4},{7,5},{8,10},{9,11},{10,... | collective-permute-start | bytes 98312 | tf_op jit(solution)/shard_map/ppermute | solution.py:499
  104.9 9.8 %collective-permute-start.13 = (bf16[144,512]{1,0:T(8,128)(2,1)}, bf16[144,512]{1,0:T(8,128)(2,1)S(1)}, u32[]{:S(2)}, u32[]{:S(2)}) collective-permute-start(bf16[144,512]{1,0:T(8,128)(2,1)} %get-tuple-element.150), channel_id=1, source_target_pairs={{0,32},{32,64},{64,96},{96,128},{128,160},{160,192},{192,224},{224... | collective-permute-start | bytes 442376 | tf_op jit(solution)/shard_map/ppermute | solution.py:430
  107.6 11.0 %collective-permute-start.14 = (bf16[144,512]{1,0:T(8,128)(2,1)}, bf16[144,512]{1,0:T(8,128)(2,1)S(1)}, u32[]{:S(2)}, u32[]{:S(2)}) collective-permute-start(bf16[144,512]{1,0:T(8,128)(2,1)} %get-tuple-element.151), channel_id=1, source_target_pairs={{0,40},{8,48},{16,56},{24,32},{32,72},{40,80},{48,88},{56,64},{64,... | collective-permute-start | bytes 442376 | tf_op jit(solution)/shard_map/ppermute | solution.py:428
  114.7 18.3 %copy-start.4 = (bf16[144,512]{1,0:T(8,128)(2,1)S(1)}, bf16[144,512]{1,0:T(8,128)(2,1)}, u32[]{:S(2)}) copy-start(bf16[144,512]{1,0:T(8,128)(2,1)} %get-tuple-element.163) | copy-start | bytes 442372
  114.7 18.3 %copy-start.5 = (bf16[144,512]{1,0:T(8,128)(2,1)S(1)}, bf16[144,512]{1,0:T(8,128)(2,1)}, u32[]{:S(2)}) copy-start(bf16[144,512]{1,0:T(8,128)(2,1)} %get-tuple-element.164) | copy-start | bytes 442372
  118.7 3.6 %collective-permute-start.15 = (bf16[12,1024]{1,0:T(8,128)(2,1)S(1)}, bf16[12,1024]{1,0:T(8,128)(2,1)S(1)}, u32[]{:S(2)}, u32[]{:S(2)}) collective-permute-start(bf16[12,1024]{1,0:T(8,128)(2,1)S(1)} %pad_maximum_fusion.12), channel_id=1, source_target_pairs={{0,1},{1,0},{2,3},{3,2},{4,5},{5,4},{6,7},{7,6},{8,9},{9,8},{10,11... | collective-permute-start | bytes 73736 | tf_op jit(solution)/shard_map/ppermute | solution.py:499
  119.5 13.4 %collective-permute-start.19 = (bf16[144,512]{1,0:T(8,128)(2,1)S(1)}, bf16[144,512]{1,0:T(8,128)(2,1)S(1)}, u32[]{:S(2)}, u32[]{:S(2)}) collective-permute-start(bf16[144,512]{1,0:T(8,128)(2,1)S(1)} %copy-done.8), channel_id=1, source_target_pairs={{0,8},{8,16},{16,24},{24,0},{1,9},{9,17},{17,25},{25,1},{2,10},{10... | collective-permute-start | bytes 442376 | tf_op jit(solution)/shard_map/ppermute | solution.py:430
  119.5 5.0 %collective-permute-start.16 = (bf16[144,512]{1,0:T(8,128)(2,1)}, bf16[144,512]{1,0:T(8,128)(2,1)S(1)}, u32[]{:S(2)}, u32[]{:S(2)}) collective-permute-start(bf16[144,512]{1,0:T(8,128)(2,1)} %get-tuple-element.155), channel_id=1, source_target_pairs={{0,8},{8,16},{16,24},{24,0},{1,9},{9,17},{17,25},{25,1},{2,10},{10... | collective-permute-start | bytes 442376 | tf_op jit(solution)/shard_map/ppermute | solution.py:430
  119.5 8.8 %collective-permute-start.17 = (bf16[144,512]{1,0:T(8,128)(2,1)}, bf16[144,512]{1,0:T(8,128)(2,1)S(1)}, u32[]{:S(2)}, u32[]{:S(2)}) collective-permute-start(bf16[144,512]{1,0:T(8,128)(2,1)} %get-tuple-element.156), channel_id=1, source_target_pairs={{0,32},{32,64},{64,96},{96,128},{128,160},{160,192},{192,224},{224... | collective-permute-start | bytes 442376 | tf_op jit(solution)/shard_map/ppermute | solution.py:430
  120.2 12.5 %collective-permute-start.18 = (bf16[144,512]{1,0:T(8,128)(2,1)}, bf16[144,512]{1,0:T(8,128)(2,1)S(1)}, u32[]{:S(2)}, u32[]{:S(2)}) collective-permute-start(bf16[144,512]{1,0:T(8,128)(2,1)} %get-tuple-element.157), channel_id=1, source_target_pairs={{0,40},{8,48},{16,56},{24,32},{32,72},{40,80},{48,88},{56,64},{64,... | collective-permute-start | bytes 442376 | tf_op jit(solution)/shard_map/ppermute | solution.py:428
  (6 other events, 32.1 us)
Sparse Core Ops, SparseCore 0:
  18.2 44.7 all-gather.1

commit v3 on v1

--- a/solution.py
+++ b/solution.py
@@ -536,6 +536,9 @@
     piece, own, gain, index = halve(sums, gain, 1)
     sums, gain = round_sums([swap(piece, 1)], own, gain, index)
     grad_proj, grad_gain = sums * norm, gain * norm
+    grad_proj, grad_gain, to_row, to_both = lax.optimization_barrier(
+        (grad_proj, grad_gain, to_row, to_both)
+    )
 
     local, to_col, to_row, to_both = (
         part.reshape(square) for part in (local, to_col, to_row, to_both)

time: 136 us -> 139 us (1.022)
    ppermute x3, waiting for transfers between devices: 0.01 us -> 2.1 us  [swap(): return lax.ppermute(piece, 'dp', [(i, i ^ bit) for i in range(d)])]
  transfers between devices with their start and end apart: 18 -> 18, of which waited for: 3 -> 4; matrix products, arithmetic and copies ran while one was open for 6% -> 5% of each run, Pallas kernels for 50% -> 49%
where the time goes in v3:
time: 139 us; the launch traced here: 138 us
  Pallas kernels  68 us (49%)
  starting transfers between devices  30.3 us (22%)
  between operations  14.5 us (10%)
  waiting for transfers between devices  13.2 us (9%)
  other arithmetic  6.37 us (5%)
  local copies, waits for them, and re-layouts  5.84 us (4%)
    pallas_call x3, Pallas kernels, backward(): pl.pallas_call(backward_kernel, grid=(count,), in_specs=[pl.BlockSpec((GR...  30.1 us
    pallas_call x1, Pallas kernels, forward(): pl.pallas_call(forward_kernel, grid=(per,), in_specs=[column_block(tokens...  20.3 us
    pallas_call x1, Pallas kernels, middle(): pl.pallas_call(lambda *refs: middle_kernel(order, *refs), in_specs=[pl.Bl...  9.69 us
    ppermute x4, starting transfers between devices, shift(): lax.ppermute(value, name, [(i, (i + step) % count) for i in range(count)])  9.4 us
    ppermute x3, starting transfers between devices, swap(): return lax.ppermute(piece, 'dp', [(i, i ^ bit) for i in range(d)])  9.19 us
    ppermute x6, starting transfers between devices, plane_round(): lax.ppermute(piece, ('row', 'col'), plane_pairs(r, c, turn, n + 1))  8.56 us
    pallas_call x1, Pallas kernels, back_product(): pl.pallas_call(back_kernel, grid=(steps,), in_specs=[pl.BlockSpec(memory_...  8.03 us
    ppermute x2, waiting for transfers between devices, shift(): return lax.ppermute(value, ('row', 'col'), pairs)  7.5 us
  transfers between devices with their start and end apart: 18, of which 4 were waited for; matrix products, arithmetic and copies ran while one was open for 5% of the time, Pallas kernels for 49%

profile of v3, /device:TPU:1, one launch (start us, length us, event | category | flops | bytes accessed | tf_op | source)
XLA Modules:
  0.0 138.3 jit_solution(3085363594030052282)
XLA Ops:
  7.2 1.7 %fusion.18 = (bf16[12,12,1024]{2,1,0:T(8,128)(2,1)S(1)}, bf16[12,12,1024]{2,1,0:T(8,128)(2,1)S(1)}, bf16[12,12,1024]{2,1,0:T(8,128)(2,1)S(1)}, bf16[12,12,1024]{2,1,0:T(8,128)(2,1)S(1)}) fusion(bf16[24,24,1024]{2,1,0:T(8,128)(2,1)} %bitcast.32), kind=kLoop, calls=%fused_computation.82 | loop fusion | bytes 2359296 | tf_op jit(solution)/shard_map/slice | solution.py:437
  9.0 3.3 %collective-permute-start = (bf16[144,1024]{1,0:T(8,128)(2,1)S(1)}, bf16[144,1024]{1,0:T(8,128)(2,1)S(1)}, u32[]{:S(2)}, u32[]{:S(2)}) collective-permute-start(bf16[144,1024]{1,0:T(8,128)(2,1)S(1)} %reshape.78), channel_id=1, source_target_pairs={{0,24},{8,0},{16,8},{24,16},{1,25},{9,1},{17,9},{25,17},{2,26},{10... | collective-permute-start | bytes 884744 | tf_op jit(solution)/shard_map/ppermute | solution.py:430
  12.4 3.5 %collective-permute-start.1 = (bf16[144,1024]{1,0:T(8,128)(2,1)S(1)}, bf16[144,1024]{1,0:T(8,128)(2,1)S(1)}, u32[]{:S(2)}, u32[]{:S(2)}) collective-permute-start(bf16[144,1024]{1,0:T(8,128)(2,1)S(1)} %reshape.80), channel_id=1, source_target_pairs={{0,224},{32,0},{64,32},{96,64},{128,96},{160,128},{192,160},{224,1... | collective-permute-start | bytes 884744 | tf_op jit(solution)/shard_map/ppermute | solution.py:430
  16.0 1.3 collective-permute-start.2
  19.1 20.3 %attn_forward.1 = (bf16[32,576,512]{2,1,0:T(8,128)(2,1)}, bf16[576,2048]{1,0:T(8,128)(2,1)}, f32[576,1024]{1,0:T(8,128)}, f32[576,1024]{1,0:T(8,128)}) custom-call(bf16[576,3072]{1,0:T(8,128)(2,1)} %bitcast.20, bf16[576,3072]{1,0:T(8,128)(2,1)} %bitcast.21, bf16[576,3072]{1,0:T(8,128)(2,1)} %bitcast.22, bf16[576,128]{1,0:T(8,128)(2,1)} %fusion.hot_ref), custom_call_target="tpu_custom_call" | custom-call | flops 25600000000 | bytes 32000000 | tf_op jit(solution)/shard_map/attn_forward/pallas_call | solution.py:208
  39.6 1.4 maximum_maximum_fusion
  40.9 9.7 %middle.1 = (bf16[576,1024]{1,0:T(8,128)(2,1)}, bf16[520,1024]{1,0:T(8,128)(2,1)}, f32[512,1024]{1,0:T(8,128)}, f32[1,1024]{1,0:T(1,128)}) custom-call(s32[1]{0:T(128)} %bitcast.refs_0_.core_ref, f32[576,1024]{1,0:T(8,128)} %get-tuple-element.65.refs_1_.o_ref, bf16[1024,1024]{1,0:T(8,128)(2,1)} %refs_2_.1, bf16[576,1024]{1,0:T(8,128)(2,1)} %bitcast.33, ...), custom_call_target="tpu_custom_call" | custom-call | flops 8000000000 | bytes 16000000 | tf_op jit(solution)/shard_map/middle/pallas_call | solution.py:294
  50.6 8.3 %attn_backward.3 = (bf16[576,256]{1,0:T(8,128)(2,1)}, bf16[576,256]{1,0:T(8,128)(2,1)}, bf16[576,256]{1,0:T(8,128)(2,1)}) custom-call(bf16[32,576,512]{2,1,0:T(8,128)(2,1)} %get-tuple-element.67.p_ref, bf16[576,2048]{1,0:T(8,128)(2,1)} %get-tuple-element.68.rest_ref, bf16[576,3072]{1,0:T(8,128)(2,1)} %bitcast.23, bf16[576,3072]{1,0:T(8,128)(2,1)} %bitcast.24, ...), custom_call_target="tpu_custom_call" | custom-call | flops 7200000000 | bytes 8000000 | tf_op jit(solution)/shard_map/attn_backward/pallas_call | solution.py:235
  60.2 2.8 %collective-permute-start.5 = (bf16[136,1024]{1,0:T(8,128)(2,1)S(1)}, bf16[136,1024]{1,0:T(8,128)(2,1)S(1)}, u32[]{:S(2)}, u32[]{:S(2)}) collective-permute-start(bf16[136,1024]{1,0:T(8,128)(2,1)S(1)} %get-tuple-element.82), channel_id=1, source_target_pairs={{0,128},{8,40},{16,144},{24,56},{32,160},{40,8},{48,176},{56,24},{... | collective-permute-start | bytes 835592 | tf_op jit(solution)/shard_map/ppermute | solution.py:486
  63.0 1.6 %collective-permute-start.6 = (bf16[136,1024]{1,0:T(8,128)(2,1)S(1)}, bf16[136,1024]{1,0:T(8,128)(2,1)S(1)}, u32[]{:S(2)}, u32[]{:S(2)}) collective-permute-start(bf16[136,1024]{1,0:T(8,128)(2,1)S(1)} %get-tuple-element.83), channel_id=1, source_target_pairs={{0,192},{8,56},{16,208},{24,8},{32,224},{40,24},{48,240},{56,40},{... | collective-permute-start | bytes 835592 | tf_op jit(solution)/shard_map/ppermute | solution.py:486
  64.6 10.9 %attn_backward.4 = (bf16[576,384]{1,0:T(8,128)(2,1)}, bf16[576,384]{1,0:T(8,128)(2,1)}, bf16[576,384]{1,0:T(8,128)(2,1)}) custom-call(bf16[32,576,512]{2,1,0:T(8,128)(2,1)} %get-tuple-element.67.p_ref, bf16[576,2048]{1,0:T(8,128)(2,1)} %get-tuple-element.68.rest_ref, bf16[576,3072]{1,0:T(8,128)(2,1)} %bitcast.26, bf16[576,3072]{1,0:T(8,128)(2,1)} %bitcast.27, ...), custom_call_target="tpu_custom_call" | custom-call | flops 10800000000 | bytes 12000000 | tf_op jit(solution)/shard_map/attn_backward/pallas_call | solution.py:235
  76.2 1.7 %collective-permute-start.8 = (bf16[40,1024]{1,0:T(8,128)(2,1)S(1)}, bf16[40,1024]{1,0:T(8,128)(2,1)S(1)}, u32[]{:S(2)}, u32[]{:S(2)}) collective-permute-start(bf16[40,1024]{1,0:T(8,128)(2,1)S(1)} %get-tuple-element.92), channel_id=1, source_target_pairs={{0,32},{8,136},{16,48},{24,152},{32,0},{40,168},{48,16},{56,184},{... | collective-permute-start | bytes 245768 | tf_op jit(solution)/shard_map/ppermute | solution.py:486
  77.9 2.0 %collective-permute-start.9 = (bf16[40,1024]{1,0:T(8,128)(2,1)S(1)}, bf16[40,1024]{1,0:T(8,128)(2,1)S(1)}, u32[]{:S(2)}, u32[]{:S(2)}) collective-permute-start(bf16[40,1024]{1,0:T(8,128)(2,1)S(1)} %get-tuple-element.93), channel_id=1, source_target_pairs={{0,48},{8,200},{16,0},{24,216},{32,16},{40,232},{48,32},{56,248},{... | collective-permute-start | bytes 245768 | tf_op jit(solution)/shard_map/ppermute | solution.py:486
  79.9 10.9 %attn_backward.5 = (bf16[576,384]{1,0:T(8,128)(2,1)}, bf16[576,384]{1,0:T(8,128)(2,1)}, bf16[576,384]{1,0:T(8,128)(2,1)}) custom-call(bf16[32,576,512]{2,1,0:T(8,128)(2,1)} %get-tuple-element.67.p_ref, bf16[576,2048]{1,0:T(8,128)(2,1)} %get-tuple-element.68.rest_ref, bf16[576,3072]{1,0:T(8,128)(2,1)} %bitcast.29, bf16[576,3072]{1,0:T(8,128)(2,1)} %bitcast.30, ...), custom_call_target="tpu_custom_call" | custom-call | flops 10800000000 | bytes 12000000 | tf_op jit(solution)/shard_map/attn_backward/pallas_call | solution.py:235
  91.1 7.0 %collective-permute-start.11 = (bf16[24,1024]{1,0:T(8,128)(2,1)S(1)}, bf16[24,1024]{1,0:T(8,128)(2,1)S(1)}, u32[]{:S(2)}, u32[]{:S(2)}) collective-permute-start(bf16[24,1024]{1,0:T(8,128)(2,1)S(1)} %pad_maximum_fusion.6), channel_id=1, source_target_pairs={{0,4},{1,5},{2,6},{3,7},{4,0},{5,1},{6,2},{7,3},{8,12},{9,13},{10,... | collective-permute-start | bytes 147464 | tf_op jit(solution)/shard_map/ppermute | solution.py:499
  98.1 8.0 %back_product.1 = (bf16[144,1024]{1,0:T(8,128)(2,1)}, bf16[144,1024]{1,0:T(8,128)(2,1)}, bf16[144,1024]{1,0:T(8,128)(2,1)}, bf16[144,1024]{1,0:T(8,128)(2,1)}) custom-call(s32[1]{0:T(128)} %bitcast.refs_0_.core_ref, bf16[576,256]{1,0:T(8,128)(2,1)} %get-tuple-element.97.refs_0_, bf16[576,384]{1,0:T(8,128)(2,1)} %get-tuple-element.98.refs_1_, ...), custom_call_target="tpu_custom_call" | custom-call | flops 6000000000 | bytes 12000000 | tf_op jit(solution)/shard_map/back_product/pallas_call | solution.py:339
  106.3 1.3 collective-permute-start.12
  107.6 1.3 collective-permute-start.13
  108.9 1.3 collective-permute-start.15
  110.2 1.7 %collective-permute-start.16 = (bf16[144,1024]{1,0:T(8,128)(2,1)}, bf16[144,1024]{1,0:T(8,128)(2,1)S(1)}, u32[]{:S(2)}, u32[]{:S(2)}) collective-permute-start(bf16[144,1024]{1,0:T(8,128)(2,1)} %get-tuple-element.118), channel_id=1, source_target_pairs={{0,40},{8,48},{16,56},{24,32},{32,72},{40,80},{48,88},{56,64},{64,... | collective-permute-start | bytes 884744 | tf_op jit(solution)/shard_map/ppermute | solution.py:428
  114.8 2.1 %collective-permute-done.14 = bf16[12,1024]{1,0:T(8,128)(2,1)S(1)} collective-permute-done((bf16[12,1024]{1,0:T(8,128)(2,1)S(1)}, bf16[12,1024]{1,0:T(8,128)(2,1)S(1)}, u32[]{:S(2)}, u32[]{:S(2)}) %collective-permute-start.14) | collective-permute-done | bytes 24608 | tf_op jit(solution)/shard_map/ppermute | solution.py:499
  118.1 3.0 %collective-permute-done.15 = bf16[144,1024]{1,0:T(8,128)(2,1)} collective-permute-done((bf16[144,1024]{1,0:T(8,128)(2,1)}, bf16[144,1024]{1,0:T(8,128)(2,1)}, u32[]{:S(2)}, u32[]{:S(2)}) %collective-permute-start.15) | collective-permute-done | bytes 294944 | tf_op jit(solution)/shard_map/ppermute | solution.py:430
  121.2 7.5 %collective-permute-done.16 = bf16[144,1024]{1,0:T(8,128)(2,1)S(1)} collective-permute-done((bf16[144,1024]{1,0:T(8,128)(2,1)}, bf16[144,1024]{1,0:T(8,128)(2,1)S(1)}, u32[]{:S(2)}, u32[]{:S(2)}) %collective-permute-start.16) | collective-permute-done | bytes 294944 | tf_op jit(solution)/shard_map/ppermute | solution.py:428
  129.9 1.5 %add_convert_fusion = bf16[1,24,24,1024]{3,2,1,0:T(8,128)(2,1)} fusion(bf16[1,24,24,1024]{3,2,1,0:T(8,128)(2,1)S(1)} %copy-done.2, bf16[1,12,24,1024]{3,2,1,0:T(8,128)(2,1)S(1)} %maximum_bitcast_fusion.1, bf16[1,12,24,1024]{3,2,1,0:T(8,128)(2,1)S(1)} %maximum_bitcast_fusion), kind=kLoop, calls=%fused_computation | loop fusion | flops 2949120 | bytes 3538944 | tf_op jit(solution)/shard_map/convert_element_type | solution.py:553
  (92 shorter events, 9.7 us)
Async XLA Ops:
  7.2 10.1 %copy-start = (bf16[128,3072]{1,0:T(8,128)(2,1)S(1)}, bf16[128,3072]{1,0:T(8,128)(2,1)}, u32[]{:S(2)}) copy-start(bf16[128,3072]{1,0:T(8,128)(2,1)} %param.8) | copy-start | bytes 2359300
  7.2 68.7 %all-gather.2.cloned.1.call-start = ((), (), s32[]{:S(2)}) async-start(), calls=%async_computation | async-start | bytes 3538944 | tf_op jit(solution)/shard_map/all_gather | solution.py:454
  9.0 9.2 %copy-start.4 = (s32[24,24]{1,0:T(8,128)S(1)}, s32[24,24]{1,0:T(8,128)}, u32[]{:S(2)}) copy-start(s32[24,24]{1,0:T(8,128)} %param.11) | copy-start | bytes 6916
  9.0 30.3 %collective-permute-start = (bf16[144,1024]{1,0:T(8,128)(2,1)S(1)}, bf16[144,1024]{1,0:T(8,128)(2,1)S(1)}, u32[]{:S(2)}, u32[]{:S(2)}) collective-permute-start(bf16[144,1024]{1,0:T(8,128)(2,1)S(1)} %reshape.78), channel_id=1, source_target_pairs={{0,24},{8,0},{16,8},{24,16},{1,25},{9,1},{17,9},{25,17},{2,26},{10... | collective-permute-start | bytes 884744 | tf_op jit(solution)/shard_map/ppermute | solution.py:430
  12.4 27.0 %collective-permute-start.1 = (bf16[144,1024]{1,0:T(8,128)(2,1)S(1)}, bf16[144,1024]{1,0:T(8,128)(2,1)S(1)}, u32[]{:S(2)}, u32[]{:S(2)}) collective-permute-start(bf16[144,1024]{1,0:T(8,128)(2,1)S(1)} %reshape.80), channel_id=1, source_target_pairs={{0,224},{32,0},{64,32},{96,64},{128,96},{160,128},{192,160},{224,1... | collective-permute-start | bytes 884744 | tf_op jit(solution)/shard_map/ppermute | solution.py:430
  16.0 23.5 %collective-permute-start.2 = (bf16[144,1024]{1,0:T(8,128)(2,1)S(1)}, bf16[144,1024]{1,0:T(8,128)(2,1)S(1)}, u32[]{:S(2)}, u32[]{:S(2)}) collective-permute-start(bf16[144,1024]{1,0:T(8,128)(2,1)S(1)} %reshape.82), channel_id=1, source_target_pairs={{0,248},{8,224},{16,232},{24,240},{32,24},{40,0},{48,8},{56,16},{6... | collective-permute-start | bytes 884744 | tf_op jit(solution)/shard_map/ppermute | solution.py:428
  50.6 8.4 %collective-permute-start.3 = (bf16[520,1024]{1,0:T(8,128)(2,1)}, bf16[520,1024]{1,0:T(8,128)(2,1)S(1)}, u32[]{:S(2)}, u32[]{:S(2)}) collective-permute-start(bf16[520,1024]{1,0:T(8,128)(2,1)} %get-tuple-element.74), channel_id=1, source_target_pairs={{0,8},{8,0},{16,24},{24,16},{1,9},{9,1},{17,25},{25,17},{2,10},{10... | collective-permute-start | bytes 3194888 | tf_op jit(solution)/shard_map/ppermute | solution.py:481
  50.6 8.3 %copy-start.3 = (f32[512,1024]{1,0:T(8,128)S(1)}, f32[512,1024]{1,0:T(8,128)}, u32[]{:S(2)}) copy-start(f32[512,1024]{1,0:T(8,128)} %get-tuple-element.66) | copy-start | bytes 6291460
  59.0 0.7 copy-start.5
  59.9 15.6 %collective-permute-start.4 = (bf16[136,1024]{1,0:T(8,128)(2,1)S(1)}, bf16[136,1024]{1,0:T(8,128)(2,1)S(1)}, u32[]{:S(2)}, u32[]{:S(2)}) collective-permute-start(bf16[136,1024]{1,0:T(8,128)(2,1)S(1)} %get-tuple-element.81), channel_id=1, source_target_pairs={{0,64},{8,24},{16,80},{24,40},{32,96},{40,56},{48,112},{56,8},{64,... | collective-permute-start | bytes 835592 | tf_op jit(solution)/shard_map/ppermute | solution.py:486
  60.2 15.3 %collective-permute-start.5 = (bf16[136,1024]{1,0:T(8,128)(2,1)S(1)}, bf16[136,1024]{1,0:T(8,128)(2,1)S(1)}, u32[]{:S(2)}, u32[]{:S(2)}) collective-permute-start(bf16[136,1024]{1,0:T(8,128)(2,1)S(1)} %get-tuple-element.82), channel_id=1, source_target_pairs={{0,128},{8,40},{16,144},{24,56},{32,160},{40,8},{48,176},{56,24},{... | collective-permute-start | bytes 835592 | tf_op jit(solution)/shard_map/ppermute | solution.py:486
  63.0 12.5 %collective-permute-start.6 = (bf16[136,1024]{1,0:T(8,128)(2,1)S(1)}, bf16[136,1024]{1,0:T(8,128)(2,1)S(1)}, u32[]{:S(2)}, u32[]{:S(2)}) collective-permute-start(bf16[136,1024]{1,0:T(8,128)(2,1)S(1)} %get-tuple-element.83), channel_id=1, source_target_pairs={{0,192},{8,56},{16,208},{24,8},{32,224},{40,24},{48,240},{56,40},{... | collective-permute-start | bytes 835592 | tf_op jit(solution)/shard_map/ppermute | solution.py:486
  75.8 22.3 %collective-permute-start.10 = (bf16[512,3072]{1,0:T(8,128)(2,1)}, bf16[512,3072]{1,0:T(8,128)(2,1)}, u32[]{:S(2)}, u32[]{:S(2)}) collective-permute-start(bf16[512,3072]{1,0:T(8,128)(2,1)} %all-gather.2.cloned.1.call-done.refs_9_), channel_id=1, source_target_pairs={{0,8},{8,0},{16,24},{24,16},{1,9},{9,1},{17,25},{25,17},{2,10},{10... | collective-permute-start | bytes 9437192 | tf_op jit(solution)/shard_map/ppermute | solution.py:479
  76.1 14.7 %collective-permute-start.7 = (bf16[40,1024]{1,0:T(8,128)(2,1)S(1)}, bf16[40,1024]{1,0:T(8,128)(2,1)S(1)}, u32[]{:S(2)}, u32[]{:S(2)}) collective-permute-start(bf16[40,1024]{1,0:T(8,128)(2,1)S(1)} %get-tuple-element.91), channel_id=1, source_target_pairs={{0,16},{8,72},{16,32},{24,88},{32,48},{40,104},{48,0},{56,120},{64... | collective-permute-start | bytes 245768 | tf_op jit(solution)/shard_map/ppermute | solution.py:486
  76.2 14.6 %collective-permute-start.8 = (bf16[40,1024]{1,0:T(8,128)(2,1)S(1)}, bf16[40,1024]{1,0:T(8,128)(2,1)S(1)}, u32[]{:S(2)}, u32[]{:S(2)}) collective-permute-start(bf16[40,1024]{1,0:T(8,128)(2,1)S(1)} %get-tuple-element.92), channel_id=1, source_target_pairs={{0,32},{8,136},{16,48},{24,152},{32,0},{40,168},{48,16},{56,184},{... | collective-permute-start | bytes 245768 | tf_op jit(solution)/shard_map/ppermute | solution.py:486
  77.9 12.9 %collective-permute-start.9 = (bf16[40,1024]{1,0:T(8,128)(2,1)S(1)}, bf16[40,1024]{1,0:T(8,128)(2,1)S(1)}, u32[]{:S(2)}, u32[]{:S(2)}) collective-permute-start(bf16[40,1024]{1,0:T(8,128)(2,1)S(1)} %get-tuple-element.93), channel_id=1, source_target_pairs={{0,48},{8,200},{16,0},{24,216},{32,16},{40,232},{48,32},{56,248},{... | collective-permute-start | bytes 245768 | tf_op jit(solution)/shard_map/ppermute | solution.py:486
  91.1 15.0 %collective-permute-start.11 = (bf16[24,1024]{1,0:T(8,128)(2,1)S(1)}, bf16[24,1024]{1,0:T(8,128)(2,1)S(1)}, u32[]{:S(2)}, u32[]{:S(2)}) collective-permute-start(bf16[24,1024]{1,0:T(8,128)(2,1)S(1)} %pad_maximum_fusion.6), channel_id=1, source_target_pairs={{0,4},{1,5},{2,6},{3,7},{4,0},{5,1},{6,2},{7,3},{8,12},{9,13},{10,... | collective-permute-start | bytes 147464 | tf_op jit(solution)/shard_map/ppermute | solution.py:499
  106.3 6.6 %collective-permute-start.12 = (bf16[16,1024]{1,0:T(8,128)(2,1)S(1)}, bf16[16,1024]{1,0:T(8,128)(2,1)S(1)}, u32[]{:S(2)}, u32[]{:S(2)}) collective-permute-start(bf16[16,1024]{1,0:T(8,128)(2,1)S(1)} %pad_maximum_fusion.7), channel_id=1, source_target_pairs={{0,2},{1,3},{2,0},{3,1},{4,6},{5,7},{6,4},{7,5},{8,10},{9,11},{10,... | collective-permute-start | bytes 98312 | tf_op jit(solution)/shard_map/ppermute | solution.py:499
  107.6 6.0 %collective-permute-start.13 = (bf16[144,1024]{1,0:T(8,128)(2,1)}, bf16[144,1024]{1,0:T(8,128)(2,1)S(1)}, u32[]{:S(2)}, u32[]{:S(2)}) collective-permute-start(bf16[144,1024]{1,0:T(8,128)(2,1)} %get-tuple-element.115), channel_id=1, source_target_pairs={{0,8},{8,16},{16,24},{24,0},{1,9},{9,17},{17,25},{25,1},{2,10},{10... | collective-permute-start | bytes 884744 | tf_op jit(solution)/shard_map/ppermute | solution.py:430
  108.9 12.2 %collective-permute-start.15 = (bf16[144,1024]{1,0:T(8,128)(2,1)}, bf16[144,1024]{1,0:T(8,128)(2,1)}, u32[]{:S(2)}, u32[]{:S(2)}) collective-permute-start(bf16[144,1024]{1,0:T(8,128)(2,1)} %get-tuple-element.117), channel_id=1, source_target_pairs={{0,32},{32,64},{64,96},{96,128},{128,160},{160,192},{192,224},{224... | collective-permute-start | bytes 884744 | tf_op jit(solution)/shard_map/ppermute | solution.py:430
  110.2 18.4 %collective-permute-start.16 = (bf16[144,1024]{1,0:T(8,128)(2,1)}, bf16[144,1024]{1,0:T(8,128)(2,1)S(1)}, u32[]{:S(2)}, u32[]{:S(2)}) collective-permute-start(bf16[144,1024]{1,0:T(8,128)(2,1)} %get-tuple-element.118), channel_id=1, source_target_pairs={{0,40},{8,48},{16,56},{24,32},{32,72},{40,80},{48,88},{56,64},{64,... | collective-permute-start | bytes 884744 | tf_op jit(solution)/shard_map/ppermute | solution.py:428
  113.6 3.3 %collective-permute-start.14 = (bf16[12,1024]{1,0:T(8,128)(2,1)S(1)}, bf16[12,1024]{1,0:T(8,128)(2,1)S(1)}, u32[]{:S(2)}, u32[]{:S(2)}) collective-permute-start(bf16[12,1024]{1,0:T(8,128)(2,1)S(1)} %pad_maximum_fusion.8), channel_id=1, source_target_pairs={{0,1},{1,0},{2,3},{3,2},{4,5},{5,4},{6,7},{7,6},{8,9},{9,8},{10,11... | collective-permute-start | bytes 73736 | tf_op jit(solution)/shard_map/ppermute | solution.py:499
  114.6 15.3 %copy-start.2 = (bf16[1,24,24,1024]{3,2,1,0:T(8,128)(2,1)S(1)}, bf16[1,24,24,1024]{3,2,1,0:T(8,128)(2,1)}, u32[]{:S(2)}) copy-start(bf16[1,24,24,1024]{3,2,1,0:T(8,128)(2,1)} %param.7) | copy-start | bytes 3538948
  129.8 1.7 %copy-start.1 = (bf16[128,3072]{1,0:T(8,128)(2,1)S(1)}, bf16[128,3072]{1,0:T(8,128)(2,1)}, u32[]{:S(2)}) copy-start(bf16[128,3072]{1,0:T(8,128)(2,1)} %param.8) | copy-start | bytes 2359300
Sparse Core Ops, SparseCore 0:
  18.2 44.7 all-gather.1

commit v4 on v1

--- a/solution.py
+++ b/solution.py
@@ -536,6 +536,7 @@
     piece, own, gain, index = halve(sums, gain, 1)
     sums, gain = round_sums([swap(piece, 1)], own, gain, index)
     grad_proj, grad_gain = sums * norm, gain * norm
+    grad, grad_proj, grad_gain = lax.optimization_barrier((grad, grad_proj, grad_gain))
 
     local, to_col, to_row, to_both = (
         part.reshape(square) for part in (local, to_col, to_row, to_both)

time: 136 us -> 147 us (1.081)
  other arithmetic: 6.38 us -> 13.9 us
  local copies, waits for them, and re-layouts: 4.88 us -> 7.5 us
    add x6, other arithmetic: 0.05 us -> 2.43 us  [round_sums(): gains.append(value[0:1].astype(F32) + value[1:2].astype(F32))]
    broadcast_in_dim x0 -> x1, other arithmetic: none -> 1.65 us  [per_device(): grad_in = (grad.astype(F32) + moved.astype(F32)).astype(BF)[None]]
    ppermute x2, waiting for transfers between devices: 8.07 us -> 6.49 us  [shift(): return lax.ppermute(value, ('row', 'col'), pairs)]
    mul x2, other arithmetic: 1.22 us -> 2.78 us  [per_device(): grad_proj, grad_gain = (sums * norm, gain * norm)]
    convert_element_type x1 -> x0, other arithmetic: 1.49 us -> none  [per_device(): grad_in = (grad.astype(F32) + moved.astype(F32)).astype(BF)[None]]
  transfers between devices with their start and end apart: 18 -> 18, of which waited for: 3 -> 3; matrix products, arithmetic and copies ran while one was open for 6% -> 10% of each run, Pallas kernels for 50% -> 47%
where the time goes in v4:
time: 147 us; the launch traced here: 146 us
  Pallas kernels  68.1 us (46%)
  starting transfers between devices  29.3 us (20%)
  between operations  14.5 us (10%)
  other arithmetic  13.9 us (9%)
  waiting for transfers between devices  12.4 us (8%)
  local copies, waits for them, and re-layouts  7.5 us (5%)
    pallas_call x3, Pallas kernels, backward(): pl.pallas_call(backward_kernel, grid=(count,), in_specs=[pl.BlockSpec((GR...  30.1 us
    pallas_call x1, Pallas kernels, forward(): pl.pallas_call(forward_kernel, grid=(per,), in_specs=[column_block(tokens...  20.3 us
    pallas_call x1, Pallas kernels, middle(): pl.pallas_call(lambda *refs: middle_kernel(order, *refs), in_specs=[pl.Bl...  9.71 us
    ppermute x4, starting transfers between devices, shift(): lax.ppermute(value, name, [(i, (i + step) % count) for i in range(count)])  9.25 us
    ppermute x3, starting transfers between devices, swap(): return lax.ppermute(piece, 'dp', [(i, i ^ bit) for i in range(d)])  9.05 us
    ppermute x6, starting transfers between devices, plane_round(): lax.ppermute(piece, ('row', 'col'), plane_pairs(r, c, turn, n + 1))  8.56 us
    pallas_call x1, Pallas kernels, back_product(): pl.pallas_call(back_kernel, grid=(steps,), in_specs=[pl.BlockSpec(memory_...  8.04 us
    ppermute x2, waiting for transfers between devices, shift(): return lax.ppermute(value, ('row', 'col'), pairs)  6.49 us
  transfers between devices with their start and end apart: 18, of which 3 were waited for; matrix products, arithmetic and copies ran while one was open for 10% of the time, Pallas kernels for 47%

profile of v4, /device:TPU:1, one launch (start us, length us, event | category | flops | bytes accessed | tf_op | source)
XLA Modules:
  0.0 145.6 jit_solution(8146456948860368468)
XLA Ops:
  7.2 1.7 %fusion.19 = (bf16[12,12,1024]{2,1,0:T(8,128)(2,1)S(1)}, bf16[12,12,1024]{2,1,0:T(8,128)(2,1)S(1)}, bf16[12,12,1024]{2,1,0:T(8,128)(2,1)S(1)}, bf16[12,12,1024]{2,1,0:T(8,128)(2,1)S(1)}) fusion(bf16[24,24,1024]{2,1,0:T(8,128)(2,1)} %bitcast.30), kind=kLoop, calls=%fused_computation.81 | loop fusion | bytes 2359296 | tf_op jit(solution)/shard_map/slice | solution.py:437
  9.0 3.3 %collective-permute-start = (bf16[144,1024]{1,0:T(8,128)(2,1)S(1)}, bf16[144,1024]{1,0:T(8,128)(2,1)S(1)}, u32[]{:S(2)}, u32[]{:S(2)}) collective-permute-start(bf16[144,1024]{1,0:T(8,128)(2,1)S(1)} %reshape.49), channel_id=1, source_target_pairs={{0,24},{8,0},{16,8},{24,16},{1,25},{9,1},{17,9},{25,17},{2,26},{10... | collective-permute-start | bytes 884744 | tf_op jit(solution)/shard_map/ppermute | solution.py:430
  12.4 3.5 %collective-permute-start.1 = (bf16[144,1024]{1,0:T(8,128)(2,1)S(1)}, bf16[144,1024]{1,0:T(8,128)(2,1)S(1)}, u32[]{:S(2)}, u32[]{:S(2)}) collective-permute-start(bf16[144,1024]{1,0:T(8,128)(2,1)S(1)} %reshape.51), channel_id=1, source_target_pairs={{0,224},{32,0},{64,32},{96,64},{128,96},{160,128},{192,160},{224,1... | collective-permute-start | bytes 884744 | tf_op jit(solution)/shard_map/ppermute | solution.py:430
  16.0 1.3 collective-permute-start.2
  19.0 20.3 %attn_forward.1 = (bf16[32,576,512]{2,1,0:T(8,128)(2,1)}, bf16[576,2048]{1,0:T(8,128)(2,1)}, f32[576,1024]{1,0:T(8,128)}, f32[576,1024]{1,0:T(8,128)}) custom-call(bf16[576,3072]{1,0:T(8,128)(2,1)} %bitcast.18, bf16[576,3072]{1,0:T(8,128)(2,1)} %bitcast.19, bf16[576,3072]{1,0:T(8,128)(2,1)} %bitcast.20, bf16[576,128]{1,0:T(8,128)(2,1)} %fusion.1.hot_ref), custom_call_target="tpu_custom_call" | custom-call | flops 25600000000 | bytes 32000000 | tf_op jit(solution)/shard_map/attn_forward/pallas_call | solution.py:208
  40.5 1.4 maximum_maximum_fusion
  41.9 9.7 %middle.1 = (bf16[576,1024]{1,0:T(8,128)(2,1)}, bf16[520,1024]{1,0:T(8,128)(2,1)}, f32[512,1024]{1,0:T(8,128)}, f32[1,1024]{1,0:T(1,128)}) custom-call(s32[1]{0:T(128)} %bitcast.1.refs_0_.core_ref, f32[576,1024]{1,0:T(8,128)} %get-tuple-element.64.refs_1_.o_ref, bf16[1024,1024]{1,0:T(8,128)(2,1)} %refs_2_.1, bf16[576,1024]{1,0:T(8,128)(2,1)} %bitcast.32, ...), custom_call_target="tpu_custom_call" | custom-call | flops 8000000000 | bytes 16000000 | tf_op jit(solution)/shard_map/middle/pallas_call | solution.py:294
  51.6 8.3 %attn_backward.3 = (bf16[576,256]{1,0:T(8,128)(2,1)}, bf16[576,256]{1,0:T(8,128)(2,1)}, bf16[576,256]{1,0:T(8,128)(2,1)}) custom-call(bf16[32,576,512]{2,1,0:T(8,128)(2,1)} %get-tuple-element.66.p_ref, bf16[576,2048]{1,0:T(8,128)(2,1)} %get-tuple-element.67.rest_ref, bf16[576,3072]{1,0:T(8,128)(2,1)} %bitcast.21, bf16[576,3072]{1,0:T(8,128)(2,1)} %bitcast.22, ...), custom_call_target="tpu_custom_call" | custom-call | flops 7200000000 | bytes 8000000 | tf_op jit(solution)/shard_map/attn_backward/pallas_call | solution.py:235
  60.9 1.5 %convert_add_fusion = f32[512,1024]{1,0:T(8,128)S(1)} fusion(f32[512,1024]{1,0:T(8,128)S(1)} %copy-done.2, bf16[520,1024]{1,0:T(8,128)(2,1)} %copy-done.3), kind=kLoop, calls=%fused_computation.1 | loop fusion | flops 1048576 | bytes 5242880 | tf_op jit(solution)/shard_map/add | solution.py:504
  63.9 2.8 %collective-permute-start.5 = (bf16[136,1024]{1,0:T(8,128)(2,1)S(1)}, bf16[136,1024]{1,0:T(8,128)(2,1)}, u32[]{:S(2)}, u32[]{:S(2)}) collective-permute-start(bf16[136,1024]{1,0:T(8,128)(2,1)S(1)} %get-tuple-element.81), channel_id=1, source_target_pairs={{0,128},{8,40},{16,144},{24,56},{32,160},{40,8},{48,176},{56,24},{... | collective-permute-start | bytes 835592 | tf_op jit(solution)/shard_map/ppermute | solution.py:486
  66.7 1.6 %collective-permute-start.6 = (bf16[136,1024]{1,0:T(8,128)(2,1)S(1)}, bf16[136,1024]{1,0:T(8,128)(2,1)}, u32[]{:S(2)}, u32[]{:S(2)}) collective-permute-start(bf16[136,1024]{1,0:T(8,128)(2,1)S(1)} %get-tuple-element.82), channel_id=1, source_target_pairs={{0,192},{8,56},{16,208},{24,8},{32,224},{40,24},{48,240},{56,40},{... | collective-permute-start | bytes 835592 | tf_op jit(solution)/shard_map/ppermute | solution.py:486
  68.4 10.8 %attn_backward.4 = (bf16[576,384]{1,0:T(8,128)(2,1)}, bf16[576,384]{1,0:T(8,128)(2,1)}, bf16[576,384]{1,0:T(8,128)(2,1)}) custom-call(bf16[32,576,512]{2,1,0:T(8,128)(2,1)} %get-tuple-element.66.p_ref, bf16[576,2048]{1,0:T(8,128)(2,1)} %get-tuple-element.67.rest_ref, bf16[576,3072]{1,0:T(8,128)(2,1)} %bitcast.24, bf16[576,3072]{1,0:T(8,128)(2,1)} %bitcast.25, ...), custom_call_target="tpu_custom_call" | custom-call | flops 10800000000 | bytes 12000000 | tf_op jit(solution)/shard_map/attn_backward/pallas_call | solution.py:235
  83.4 1.7 %collective-permute-start.8 = (bf16[40,1024]{1,0:T(8,128)(2,1)S(1)}, bf16[40,1024]{1,0:T(8,128)(2,1)S(1)}, u32[]{:S(2)}, u32[]{:S(2)}) collective-permute-start(bf16[40,1024]{1,0:T(8,128)(2,1)S(1)} %get-tuple-element.91), channel_id=1, source_target_pairs={{0,32},{8,136},{16,48},{24,152},{32,0},{40,168},{48,16},{56,184},{... | collective-permute-start | bytes 245768 | tf_op jit(solution)/shard_map/ppermute | solution.py:486
  85.1 2.0 %collective-permute-start.9 = (bf16[40,1024]{1,0:T(8,128)(2,1)S(1)}, bf16[40,1024]{1,0:T(8,128)(2,1)S(1)}, u32[]{:S(2)}, u32[]{:S(2)}) collective-permute-start(bf16[40,1024]{1,0:T(8,128)(2,1)S(1)} %get-tuple-element.92), channel_id=1, source_target_pairs={{0,48},{8,200},{16,0},{24,216},{32,16},{40,232},{48,32},{56,248},{... | collective-permute-start | bytes 245768 | tf_op jit(solution)/shard_map/ppermute | solution.py:486
  87.1 10.9 %attn_backward.5 = (bf16[576,384]{1,0:T(8,128)(2,1)}, bf16[576,384]{1,0:T(8,128)(2,1)}, bf16[576,384]{1,0:T(8,128)(2,1)}) custom-call(bf16[32,576,512]{2,1,0:T(8,128)(2,1)} %get-tuple-element.66.p_ref, bf16[576,2048]{1,0:T(8,128)(2,1)} %get-tuple-element.67.rest_ref, bf16[576,3072]{1,0:T(8,128)(2,1)} %bitcast.27, bf16[576,3072]{1,0:T(8,128)(2,1)} %bitcast.28, ...), custom_call_target="tpu_custom_call" | custom-call | flops 10800000000 | bytes 12000000 | tf_op jit(solution)/shard_map/attn_backward/pallas_call | solution.py:235
  98.3 7.0 %collective-permute-start.11 = (bf16[24,1024]{1,0:T(8,128)(2,1)S(1)}, bf16[24,1024]{1,0:T(8,128)(2,1)S(1)}, u32[]{:S(2)}, u32[]{:S(2)}) collective-permute-start(bf16[24,1024]{1,0:T(8,128)(2,1)S(1)} %pad_maximum_fusion.6), channel_id=1, source_target_pairs={{0,4},{1,5},{2,6},{3,7},{4,0},{5,1},{6,2},{7,3},{8,12},{9,13},{10,... | collective-permute-start | bytes 147464 | tf_op jit(solution)/shard_map/ppermute | solution.py:499
  105.3 8.0 %back_product.1 = (bf16[144,1024]{1,0:T(8,128)(2,1)}, bf16[144,1024]{1,0:T(8,128)(2,1)}, bf16[144,1024]{1,0:T(8,128)(2,1)}, bf16[144,1024]{1,0:T(8,128)(2,1)}) custom-call(s32[1]{0:T(128)} %bitcast.1.refs_0_.core_ref, bf16[576,256]{1,0:T(8,128)(2,1)} %get-tuple-element.96.refs_0_, bf16[576,384]{1,0:T(8,128)(2,1)} %get-tuple-element.97.refs_1_, ...), custom_call_target="tpu_custom_call" | custom-call | flops 6000000000 | bytes 12000000 | tf_op jit(solution)/shard_map/back_product/pallas_call | solution.py:339
  114.8 1.3 collective-permute-start.13
  118.4 3.0 %collective-permute-done.13 = bf16[144,1024]{1,0:T(8,128)(2,1)S(1)} collective-permute-done((bf16[144,1024]{1,0:T(8,128)(2,1)}, bf16[144,1024]{1,0:T(8,128)(2,1)S(1)}, u32[]{:S(2)}, u32[]{:S(2)}) %collective-permute-start.13) | collective-permute-done | bytes 294944 | tf_op jit(solution)/shard_map/ppermute | solution.py:430
  123.9 6.5 %collective-permute-done.15 = bf16[144,1024]{1,0:T(8,128)(2,1)S(1)} collective-permute-done((bf16[144,1024]{1,0:T(8,128)(2,1)}, bf16[144,1024]{1,0:T(8,128)(2,1)S(1)}, u32[]{:S(2)}, u32[]{:S(2)}) %collective-permute-start.15) | collective-permute-done | bytes 294944 | tf_op jit(solution)/shard_map/ppermute | solution.py:428
  130.4 2.9 %collective-permute-done.16 = bf16[144,1024]{1,0:T(8,128)(2,1)} collective-permute-done((bf16[144,1024]{1,0:T(8,128)(2,1)}, bf16[144,1024]{1,0:T(8,128)(2,1)}, u32[]{:S(2)}, u32[]{:S(2)}) %collective-permute-start.16) | collective-permute-done | bytes 294944 | tf_op jit(solution)/shard_map/ppermute | solution.py:430
  134.4 1.4 fusion.12
  135.8 1.4 add_multiply_fusion
  137.1 1.6 %fusion = bf16[1,24,24,1024]{3,2,1,0:T(8,128)(2,1)} fusion(bf16[24,24,1024]{2,1,0:T(8,128)(2,1)S(1)} %bitcast.31, bf16[12,12,1024]{2,1,0:T(8,128)(2,1)S(1)} %reshape.59, bf16[12,12,1024]{2,1,0:T(8,128)(2,1)S(1)} %reshape.58, bf16[12,12,1024]{2,1,0:T(8,128)(2,1)S(1)} %reshape.57, bf16[12,12,1024]{2,1,0:T(8,128)(2,1)S(1)} %reshape.56), kind=kLoop, calls=%fused_computation.2 | loop fusion | flops 6488064 | bytes 3538944 | tf_op jit(solution)/shard_map/broadcast_in_dim | solution.py:551
  (92 shorter events, 17.2 us)
Async XLA Ops:
  7.2 10.1 %copy-start = (bf16[128,3072]{1,0:T(8,128)(2,1)S(1)}, bf16[128,3072]{1,0:T(8,128)(2,1)}, u32[]{:S(2)}) copy-start(bf16[128,3072]{1,0:T(8,128)(2,1)} %param.8) | copy-start | bytes 2359300
  7.2 75.8 %all-gather.2.cloned.1.call-start = ((), (), s32[]{:S(2)}) async-start(), calls=%async_computation | async-start | bytes 3538944 | tf_op jit(solution)/shard_map/all_gather | solution.py:454
  9.0 9.2 %copy-start.5 = (s32[24,24]{1,0:T(8,128)S(1)}, s32[24,24]{1,0:T(8,128)}, u32[]{:S(2)}) copy-start(s32[24,24]{1,0:T(8,128)} %param.11) | copy-start | bytes 6916
  9.0 30.3 %collective-permute-start = (bf16[144,1024]{1,0:T(8,128)(2,1)S(1)}, bf16[144,1024]{1,0:T(8,128)(2,1)S(1)}, u32[]{:S(2)}, u32[]{:S(2)}) collective-permute-start(bf16[144,1024]{1,0:T(8,128)(2,1)S(1)} %reshape.49), channel_id=1, source_target_pairs={{0,24},{8,0},{16,8},{24,16},{1,25},{9,1},{17,9},{25,17},{2,26},{10... | collective-permute-start | bytes 884744 | tf_op jit(solution)/shard_map/ppermute | solution.py:430
  12.4 27.0 %collective-permute-start.1 = (bf16[144,1024]{1,0:T(8,128)(2,1)S(1)}, bf16[144,1024]{1,0:T(8,128)(2,1)S(1)}, u32[]{:S(2)}, u32[]{:S(2)}) collective-permute-start(bf16[144,1024]{1,0:T(8,128)(2,1)S(1)} %reshape.51), channel_id=1, source_target_pairs={{0,224},{32,0},{64,32},{96,64},{128,96},{160,128},{192,160},{224,1... | collective-permute-start | bytes 884744 | tf_op jit(solution)/shard_map/ppermute | solution.py:430
  16.0 23.5 %collective-permute-start.2 = (bf16[144,1024]{1,0:T(8,128)(2,1)S(1)}, bf16[144,1024]{1,0:T(8,128)(2,1)}, u32[]{:S(2)}, u32[]{:S(2)}) collective-permute-start(bf16[144,1024]{1,0:T(8,128)(2,1)S(1)} %reshape.53), channel_id=1, source_target_pairs={{0,248},{8,224},{16,232},{24,240},{32,24},{40,0},{48,8},{56,16},{6... | collective-permute-start | bytes 884744 | tf_op jit(solution)/shard_map/ppermute | solution.py:428
  51.6 8.4 %collective-permute-start.3 = (bf16[520,1024]{1,0:T(8,128)(2,1)}, bf16[520,1024]{1,0:T(8,128)(2,1)S(1)}, u32[]{:S(2)}, u32[]{:S(2)}) collective-permute-start(bf16[520,1024]{1,0:T(8,128)(2,1)} %get-tuple-element.73), channel_id=1, source_target_pairs={{0,8},{8,0},{16,24},{24,16},{1,9},{9,1},{17,25},{25,17},{2,10},{10... | collective-permute-start | bytes 3194888 | tf_op jit(solution)/shard_map/ppermute | solution.py:481
  51.6 9.3 %copy-start.2 = (f32[512,1024]{1,0:T(8,128)S(1)}, f32[512,1024]{1,0:T(8,128)}, u32[]{:S(2)}) copy-start(f32[512,1024]{1,0:T(8,128)} %get-tuple-element.65) | copy-start | bytes 6291460
  60.9 1.7 %copy-start.6 = (f32[1,1024]{1,0:T(1,128)S(1)}, f32[1,1024]{1,0:T(1,128)}, u32[]{:S(2)}) copy-start(f32[1,1024]{1,0:T(1,128)} %get-tuple-element.75) | copy-start | bytes 12292
  63.6 15.6 %collective-permute-start.4 = (bf16[136,1024]{1,0:T(8,128)(2,1)S(1)}, bf16[136,1024]{1,0:T(8,128)(2,1)}, u32[]{:S(2)}, u32[]{:S(2)}) collective-permute-start(bf16[136,1024]{1,0:T(8,128)(2,1)S(1)} %get-tuple-element.80), channel_id=1, source_target_pairs={{0,64},{8,24},{16,80},{24,40},{32,96},{40,56},{48,112},{56,8},{64,... | collective-permute-start | bytes 835592 | tf_op jit(solution)/shard_map/ppermute | solution.py:486
  63.9 15.3 %collective-permute-start.5 = (bf16[136,1024]{1,0:T(8,128)(2,1)S(1)}, bf16[136,1024]{1,0:T(8,128)(2,1)}, u32[]{:S(2)}, u32[]{:S(2)}) collective-permute-start(bf16[136,1024]{1,0:T(8,128)(2,1)S(1)} %get-tuple-element.81), channel_id=1, source_target_pairs={{0,128},{8,40},{16,144},{24,56},{32,160},{40,8},{48,176},{56,24},{... | collective-permute-start | bytes 835592 | tf_op jit(solution)/shard_map/ppermute | solution.py:486
  66.7 12.5 %collective-permute-start.6 = (bf16[136,1024]{1,0:T(8,128)(2,1)S(1)}, bf16[136,1024]{1,0:T(8,128)(2,1)}, u32[]{:S(2)}, u32[]{:S(2)}) collective-permute-start(bf16[136,1024]{1,0:T(8,128)(2,1)S(1)} %get-tuple-element.82), channel_id=1, source_target_pairs={{0,192},{8,56},{16,208},{24,8},{32,224},{40,24},{48,240},{56,40},{... | collective-permute-start | bytes 835592 | tf_op jit(solution)/shard_map/ppermute | solution.py:486
  83.0 22.3 %collective-permute-start.10 = (bf16[512,3072]{1,0:T(8,128)(2,1)}, bf16[512,3072]{1,0:T(8,128)(2,1)}, u32[]{:S(2)}, u32[]{:S(2)}) collective-permute-start(bf16[512,3072]{1,0:T(8,128)(2,1)} %all-gather.2.cloned.1.call-done.refs_9_), channel_id=1, source_target_pairs={{0,8},{8,0},{16,24},{24,16},{1,9},{9,1},{17,25},{25,17},{2,10},{10... | collective-permute-start | bytes 9437192 | tf_op jit(solution)/shard_map/ppermute | solution.py:479
  83.3 14.7 %collective-permute-start.7 = (bf16[40,1024]{1,0:T(8,128)(2,1)S(1)}, bf16[40,1024]{1,0:T(8,128)(2,1)S(1)}, u32[]{:S(2)}, u32[]{:S(2)}) collective-permute-start(bf16[40,1024]{1,0:T(8,128)(2,1)S(1)} %get-tuple-element.90), channel_id=1, source_target_pairs={{0,16},{8,72},{16,32},{24,88},{32,48},{40,104},{48,0},{56,120},{64... | collective-permute-start | bytes 245768 | tf_op jit(solution)/shard_map/ppermute | solution.py:486
  83.4 14.6 %collective-permute-start.8 = (bf16[40,1024]{1,0:T(8,128)(2,1)S(1)}, bf16[40,1024]{1,0:T(8,128)(2,1)S(1)}, u32[]{:S(2)}, u32[]{:S(2)}) collective-permute-start(bf16[40,1024]{1,0:T(8,128)(2,1)S(1)} %get-tuple-element.91), channel_id=1, source_target_pairs={{0,32},{8,136},{16,48},{24,152},{32,0},{40,168},{48,16},{56,184},{... | collective-permute-start | bytes 245768 | tf_op jit(solution)/shard_map/ppermute | solution.py:486
  85.1 12.9 %collective-permute-start.9 = (bf16[40,1024]{1,0:T(8,128)(2,1)S(1)}, bf16[40,1024]{1,0:T(8,128)(2,1)S(1)}, u32[]{:S(2)}, u32[]{:S(2)}) collective-permute-start(bf16[40,1024]{1,0:T(8,128)(2,1)S(1)} %get-tuple-element.92), channel_id=1, source_target_pairs={{0,48},{8,200},{16,0},{24,216},{32,16},{40,232},{48,32},{56,248},{... | collective-permute-start | bytes 245768 | tf_op jit(solution)/shard_map/ppermute | solution.py:486
  98.3 15.0 %collective-permute-start.11 = (bf16[24,1024]{1,0:T(8,128)(2,1)S(1)}, bf16[24,1024]{1,0:T(8,128)(2,1)S(1)}, u32[]{:S(2)}, u32[]{:S(2)}) collective-permute-start(bf16[24,1024]{1,0:T(8,128)(2,1)S(1)} %pad_maximum_fusion.6), channel_id=1, source_target_pairs={{0,4},{1,5},{2,6},{3,7},{4,0},{5,1},{6,2},{7,3},{8,12},{9,13},{10,... | collective-permute-start | bytes 147464 | tf_op jit(solution)/shard_map/ppermute | solution.py:499
  113.3 23.8 %copy-start.1 = (bf16[1,24,24,1024]{3,2,1,0:T(8,128)(2,1)S(1)}, bf16[1,24,24,1024]{3,2,1,0:T(8,128)(2,1)}, u32[]{:S(2)}) copy-start(bf16[1,24,24,1024]{3,2,1,0:T(8,128)(2,1)} %param.7) | copy-start | bytes 3538948
  113.5 4.7 %collective-permute-start.12 = (bf16[16,1024]{1,0:T(8,128)(2,1)S(1)}, bf16[16,1024]{1,0:T(8,128)(2,1)S(1)}, u32[]{:S(2)}, u32[]{:S(2)}) collective-permute-start(bf16[16,1024]{1,0:T(8,128)(2,1)S(1)} %pad_maximum_fusion.7), channel_id=1, source_target_pairs={{0,2},{1,3},{2,0},{3,1},{4,6},{5,7},{6,4},{7,5},{8,10},{9,11},{10,... | collective-permute-start | bytes 98312 | tf_op jit(solution)/shard_map/ppermute | solution.py:499
  114.8 6.5 %collective-permute-start.13 = (bf16[144,1024]{1,0:T(8,128)(2,1)}, bf16[144,1024]{1,0:T(8,128)(2,1)S(1)}, u32[]{:S(2)}, u32[]{:S(2)}) collective-permute-start(bf16[144,1024]{1,0:T(8,128)(2,1)} %get-tuple-element.114), channel_id=1, source_target_pairs={{0,8},{8,16},{16,24},{24,0},{1,9},{9,17},{17,25},{25,1},{2,10},{10... | collective-permute-start | bytes 884744 | tf_op jit(solution)/shard_map/ppermute | solution.py:430
  116.1 14.2 %collective-permute-start.15 = (bf16[144,1024]{1,0:T(8,128)(2,1)}, bf16[144,1024]{1,0:T(8,128)(2,1)S(1)}, u32[]{:S(2)}, u32[]{:S(2)}) collective-permute-start(bf16[144,1024]{1,0:T(8,128)(2,1)} %get-tuple-element.117), channel_id=1, source_target_pairs={{0,40},{8,48},{16,56},{24,32},{32,72},{40,80},{48,88},{56,64},{64,... | collective-permute-start | bytes 884744 | tf_op jit(solution)/shard_map/ppermute | solution.py:428
  117.1 16.2 %collective-permute-start.16 = (bf16[144,1024]{1,0:T(8,128)(2,1)}, bf16[144,1024]{1,0:T(8,128)(2,1)}, u32[]{:S(2)}, u32[]{:S(2)}) collective-permute-start(bf16[144,1024]{1,0:T(8,128)(2,1)} %get-tuple-element.118), channel_id=1, source_target_pairs={{0,32},{32,64},{64,96},{96,128},{128,160},{160,192},{192,224},{224... | collective-permute-start | bytes 884744 | tf_op jit(solution)/shard_map/ppermute | solution.py:430
  118.3 5.6 %copy-start.4 = (f32[8,1024]{1,0:T(8,128)}, f32[8,1024]{1,0:T(8,128)S(1)}, u32[]{:S(2)}) copy-start(f32[8,1024]{1,0:T(8,128)S(1)} %convert_add_fusion.4) | copy-start | bytes 98308
  122.0 12.4 %collective-permute-start.14 = (bf16[12,1024]{1,0:T(8,128)(2,1)}, bf16[12,1024]{1,0:T(8,128)(2,1)}, u32[]{:S(2)}, u32[]{:S(2)}) collective-permute-start(bf16[12,1024]{1,0:T(8,128)(2,1)} %pad_maximum_fusion.8), channel_id=1, source_target_pairs={{0,1},{1,0},{2,3},{3,2},{4,5},{5,4},{6,7},{7,6},{8,9},{9,8},{10,11... | collective-permute-start | bytes 73736 | tf_op jit(solution)/shard_map/ppermute | solution.py:499
  (1 other events, 1.0 us)
Sparse Core Ops, SparseCore 0:
  18.2 44.7 all-gather.1
